TPU v7x, 32 devices: a whole 2x2x4 slice. The times are simulated.
32 devices in a mesh: run: 4 (over z), tm: 2 (over core), blk: 4 (over y, x).
Axes of the slice: x: 2, y: 2, z: 4, core: 2. Of those that a mesh axis runs over, the one named last changes fastest.
Arguments:
- series: bfloat16 [4, 1200, 6144], P('run', 'tm', 'blk'), may hold values from -60 to 60
- weights: int32 [4, 1200], P('run'), may hold values from 0 to 2
- taps: bfloat16 [33], replicated, may hold values from -3 to 3
- lags: int32 [6144], P('blk'), may hold values from 0 to 3
Outputs:
- connectome: float32 [512, 6144], P(('run', 'tm'), 'blk')
All inputs are finite; a program needn't handle non-finite values.
Results may differ from a plain program's by a relative error of at most 0.00055.
Values may be sent and summed in bfloat16 or wider, within the bound.
A program may use at most 128 MiB of HBM per device.

v0:
```python
import jax
import jax.numpy as jnp
from jax import lax
from jax.sharding import PartitionSpec as P

HALF = 16
LAGS = 4
SEED_DEV = 128


epsilon = 1e-05


def extended(array, sides, width):
    for axis, dim in sides:
        devices, length = (lax.axis_size(axis), array.shape[dim])
        up = [(i, (i + 1) % devices) for i in range(devices - 1)]
        down = [(j, i) for i, j in up]
        last = lax.slice_in_dim(array, length - width, length, axis=dim)
        initial = lax.slice_in_dim(array, 0, width, axis=dim)
        before = lax.ppermute(last, axis, up)
        after = lax.ppermute(initial, axis, down)
        array = jnp.concatenate([before, array, after], axis=dim)
    return array


def local(series, weights, taps, lags):
    signal = series[0]
    frame_count, panel_width = signal.shape
    n_run = lax.axis_size("run")
    n_blk = lax.axis_size("blk")
    tm_index = lax.axis_index("tm")
    width = HALF + LAGS
    padded = extended(signal, (("tm", 0),), width)
    out_count = frame_count + LAGS
    banded = jnp.zeros((out_count, panel_width), jnp.float32)
    for tap_index in range(2 * HALF + 1):
        start = LAGS + tap_index
        banded = banded + taps[tap_index].astype(jnp.float32) * padded[
            start : start + out_count
        ].astype(jnp.float32)
    shifted = jnp.zeros((frame_count, panel_width), jnp.float32)
    for lag_value in range(LAGS):
        shifted = jnp.where(
            lags[None, :] == lag_value, banded[lag_value : lag_value + frame_count], shifted
        )
    filtered = shifted.astype(jnp.bfloat16)
    weight_all = weights[0].astype(jnp.float32)
    weight_sum = jnp.sum(weight_all)
    weight_own = lax.dynamic_slice_in_dim(weight_all, tm_index * frame_count, frame_count)
    values = filtered.astype(jnp.float32)
    first_sum, second_sum = lax.psum(
        (
            jnp.sum(weight_own[:, None] * values, axis=0),
            jnp.sum(weight_own[:, None] * values * values, axis=0),
        ),
        "tm",
    )
    first = first_sum / weight_sum
    second = second_sum / weight_sum
    scaling = lax.rsqrt(second - first * first + epsilon)
    scores_own = (jnp.sqrt(weight_own)[:, None] * (values - first) * scaling).astype(jnp.bfloat16)
    stride = panel_width // SEED_DEV
    seed_own = scores_own[:, ::stride].T
    gathered = lax.all_gather(seed_own[:, None, :], "blk", axis=1, tiled=True)
    seed_block = gathered.reshape(SEED_DEV * n_blk, frame_count)
    summed = lax.psum_scatter(
        jnp.dot(seed_block, scores_own, preferred_element_type=jnp.float32) / weight_sum,
        ("run", "tm"),
        scatter_dimension=0,
        tiled=True,
    )
    return summed / n_run


def solution(mesh):
    placed = (P("run", "tm", "blk"), P("run", None), P(), P("blk"))
    return jax.shard_map(
        local, mesh=mesh, in_specs=placed, out_specs=P(("run", "tm"), "blk"), check_vma=False
    )
```

profile of v0, /device:TPU:0, one launch (start us, length us, event | category | flops | bytes accessed | tf_op | source)
XLA Modules:
  0.0 178.5 jit_solution(1968084474320124362)
XLA Ops:
  6.5 0.9 slice_bitcast_fusion
  7.5 1.3 collective-permute-start.1
  8.8 3.0 %collective-permute-start = (bf16[20,1536]{1,0:T(8,128)(2,1)S(1)}, bf16[20,1536]{1,0:T(8,128)(2,1)S(1)}, u32[]{:S(2)}, u32[]{:S(2)}) collective-permute-start(bf16[20,1536]{1,0:T(8,128)(2,1)S(1)} %get-tuple-element.11), channel_id=1, source_target_pairs={{0,4},{1,5},{2,6},{3,7},{8,12},{9,13},{10,14},{11,15},{16,20},{17,... | collective-permute-start | bytes 184328 | tf_op jit(solution)/shard_map/ppermute | solution.py:21
  11.8 1.9 %fusion.39 = (bf16[1]{0:T(256)(128)(2,1)}, bf16[1]{0:T(256)(128)(2,1)}, bf16[1]{0:T(256)(128)(2,1)}, bf16[1]{0:T(256)(128)(2,1)}, bf16[1]{0:T(256)(128)(2,1)}, /...) fusion(bf16[33]{0:T(256)(128)(2,1)} %param.6), kind=kLoop, calls=%fused_computation.101 | loop fusion | bytes 56 | tf_op jit(solution)/shard_map/slice | solution.py:39
  13.7 2.1 %fusion.38 = (bf16[1]{0:T(256)(128)(2,1)}, bf16[1]{0:T(256)(128)(2,1)}, bf16[1]{0:T(256)(128)(2,1)}, bf16[1]{0:T(256)(128)(2,1)}, bf16[1]{0:T(256)(128)(2,1)}, /...) fusion(bf16[33]{0:T(256)(128)(2,1)} %param.6), kind=kLoop, calls=%fused_computation.100 | loop fusion | bytes 76 | tf_op jit(solution)/shard_map/slice | solution.py:39
  15.8 0.7 convert_element_type.310
  16.5 0.1 dynamic-slice_reduce_fusion
  25.4 0.7 broadcast_compare_fusion.3
  38.1 1.3 convert_reduce_fusion
  39.4 0.0 collective-permute-done.1
  39.4 3.2 %pad_maximum_fusion = bf16[640,1536]{1,0:T(8,128)(2,1)} fusion(bf16[20,1536]{1,0:T(8,128)(2,1)S(1)} %collective-permute-done.1, bf16[600,1536]{1,0:T(8,128)(2,1)} %bitcast.74, bf16[20,1536]{1,0:T(8,128)(2,1)S(1)} %collective-permute-done), kind=kLoop, calls=%fused_computation.43 | loop fusion | flops 5898240 | bytes 3932160 | tf_op jit(solution)/shard_map/concatenate | solution.py:23
  42.6 53.4 %multiply_add_fusion = bf16[604,1536]{1,0:T(8,128)(2,1)S(1)} fusion(bf16[20,1536]{1,0:T(8,128)(2,1)S(1)} %collective-permute-done, bf16[20,1536]{1,0:T(8,128)(2,1)S(1)} %collective-permute-done.1, bf16[600,1536]{1,0:T(8,128)(2,1)} %bitcast.75, bf16[640,1536]{1,0:T(8,128)(2,1)} %pad_maximum_fusion, f32[]{:T(128)S(6)} %convert.65, f32[]{:T(128)S(6)} %convert.64, ...), kind=kLoop, calls=%fused_computation.32 | loop fusion | flops 175343616 | bytes 9388164 | tf_op jit(solution)/shard_map/add | solution.py:39
  96.0 3.2 %fusion = (f32[1536]{0:T(1024)S(1)}, f32[1536]{0:T(1024)S(1)}, bf16[600,1536]{1,0:T(8,128)(2,1)}) fusion(f32[600]{0:T(1024)S(1)} %dynamic-slice_reduce_fusion, bf16[604,1536]{1,0:T(8,128)(2,1)S(1)} %multiply_add_fusion, pred[1536]{0:T(1024)(128)(4,1)S(1)} %get-tuple-element.16, pred[1536]{0:T(1024)(128)(4,1)S(1)} %get-tuple-element.17, ...), kind=kLoop, calls=%fused_computation.31 | loop fusion | flops 8291328 | bytes 9236832 | tf_op jit(solution)/shard_map/reduce_sum | solution.py:54
  99.2 3.3 %all-reduce = (f32[1536]{0:T(1024)S(1)}, f32[1536]{0:T(1024)S(1)}) all-reduce(f32[1536]{0:T(1024)S(1)} %get-tuple-element.6, f32[1536]{0:T(1024)S(1)} %get-tuple-element.5), channel_id=1, replica_groups=mesh['run'=4,'tm'=2,'blk'=4] {'tm'}, use_global_device_ids=true, to_apply=%region_4.5 | all-reduce | flops 3072 | bytes 24576 | tf_op jit(solution)/shard_map/psum | solution.py:52
  102.5 0.7 broadcast_divide_fusion
  103.2 2.1 %fusion.3 = bf16[600,1536]{1,0:T(8,128)(2,1)S(1)} fusion(bf16[600,1536]{1,0:T(8,128)(2,1)} %get-tuple-element.9, f32[1536]{0:T(1024)S(1)} %get-tuple-element.13, f32[1536]{0:T(1024)S(1)} %get-tuple-element.12, f32[600]{0:T(1024)S(1)} %sqrt.3), kind=kLoop, calls=%fused_computation.35 | loop fusion | flops 4608000 | bytes 3701088 | tf_op jit(solution)/shard_map/convert_element_type | solution.py:62
  105.2 6.4 %slice.329 = bf16[600,128]{1,0:T(8,128)(2,1)S(1)} slice(bf16[600,1536]{1,0:T(8,128)(2,1)S(1)} %fusion.3), slice={[0:600:1], [0:1536:12]} | slice | bytes 307200 | tf_op jit(solution)/shard_map/slice | solution.py:64
  111.6 12.6 %all-gather = bf16[128,2400]{0,1:T(8,128)(2,1)S(1)} all-gather(bf16[128,600]{0,1:T(8,128)(2,1)S(1)} %bitcast.76), channel_id=2, replica_groups=mesh['run'=4,'tm'=2,'blk'=4] {'blk'}, dimensions={1}, use_global_device_ids=true | all-gather | bytes 768000 | tf_op jit(solution)/shard_map/all_gather | solution.py:65
  124.2 0.3 copy.5
  124.5 0.8 reshape.85
  125.3 3.7 %convolution_divide_fusion = f32[512,1536]{1,0:T(8,128)} fusion(bf16[512,600]{1,0:T(8,128)(2,1)S(1)} %reshape.85, bf16[600,1536]{1,0:T(8,128)(2,1)S(1)} %fusion.3, f32[]{:T(128)} %convert_reduce_fusion), kind=kOutput, calls=%fused_computation.42 | convolution fusion | flops 944504832 | bytes 5603332 | tf_op jit(solution)/shard_map/dot_general | solution.py:68
  129.0 0.0 reduce-scatter.2.cloned.1.call-update
  129.1 40.8 %reduce-scatter.2.cloned.1.call-done = f32[64,1536]{1,0:T(8,128)} async-done(((f32[512,1536]{1,0:T(8,128)}), f32[64,1536]{1,0:T(8,128)}) %reduce-scatter.2.cloned.1.call-update) | async-done | bytes 393232 | tf_op jit(solution)/shard_map/reduce_scatter | solution.py:67
  169.9 1.8 broadcast_multiply_fusion
  (3 shorter events, 0.0 us)
Async XLA Ops:
  6.5 163.3 %reduce-scatter.2.cloned.1.call-start = ((), (), s32[]{:S(2)}) async-start(), calls=%async_computation.1 | async-start | bytes 3538944 | tf_op jit(solution)/shard_map/reduce_scatter | solution.py:67
  7.5 31.9 %collective-permute-start.1 = (bf16[20,1536]{1,0:T(8,128)(2,1)S(1)}, bf16[20,1536]{1,0:T(8,128)(2,1)S(1)}, u32[]{:S(2)}, u32[]{:S(2)}) collective-permute-start(bf16[20,1536]{1,0:T(8,128)(2,1)S(1)} %get-tuple-element.10), channel_id=1, source_target_pairs={{4,0},{5,1},{6,2},{7,3},{12,8},{13,9},{14,10},{15,11},{20,16},{21,... | collective-permute-start | bytes 184328 | tf_op jit(solution)/shard_map/ppermute | solution.py:22
  8.8 30.6 %collective-permute-start = (bf16[20,1536]{1,0:T(8,128)(2,1)S(1)}, bf16[20,1536]{1,0:T(8,128)(2,1)S(1)}, u32[]{:S(2)}, u32[]{:S(2)}) collective-permute-start(bf16[20,1536]{1,0:T(8,128)(2,1)S(1)} %get-tuple-element.11), channel_id=1, source_target_pairs={{0,4},{1,5},{2,6},{3,7},{8,12},{9,13},{10,14},{11,15},{16,20},{17,... | collective-permute-start | bytes 184328 | tf_op jit(solution)/shard_map/ppermute | solution.py:21
Sparse Core Ops, SparseCore 0:
  129.2 40.6 reduce-scatter.1
where the time goes:
time: 179 us; the launch traced here: 178 us
  other arithmetic  67 us (37%)
  waiting for transfers between devices  40.8 us (23%)
  between operations  34.3 us (19%)
  blocking collectives  15.9 us (9%)
  local copies, waits for them, and re-layouts  12.4 us (7%)
  starting transfers between devices  4.33 us (2%)
  matrix products  3.71 us (2%)
    add x1, other arithmetic, local(): banded + taps[tap_index].astype(jnp.float32) * padded[start:start + out_c...  53.4 us
    reduce_scatter x1, waiting for transfers between devices, local(): lax.psum_scatter(jnp.dot(seed_block, scores_own, preferred_element_type=j...  40.8 us
    all_gather x1, blocking collectives, local(): gathered = lax.all_gather(seed_own[:, None, :], 'blk', axis=1, tiled=True)  12.6 us
    slice x1, local copies, waits for them, and re-layouts, local(): seed_own = scores_own[:, ::stride].T  6.37 us
    slice x2, local copies, waits for them, and re-layouts, local(): taps[tap_index].astype(jnp.float32)  3.96 us
    dot_general x1, matrix products, local(): jnp.dot(seed_block, scores_own, preferred_element_type=jnp.float32)  3.71 us
  transfers between devices with their start and end apart: 3, of which 1 were waited for; matrix products, arithmetic and copies ran while one was open for 4% of the time, Pallas kernels for 0%

commit v1 on v0

v1 whole, which is shorter than its diff:
```python
import functools

import jax
import jax.numpy as jnp
from jax import lax
from jax.experimental import pallas as pl
from jax.experimental.pallas import tpu as pltpu
from jax.sharding import PartitionSpec as P

HALF = 16
LAGS = 4
SEED_DEV = 128
TAPS = 2 * HALF + 1
OUT_BLK = 224
IN_BLK = 256
CHUNK = 64
TOP = 32000.0
STEPS = 128.0
epsilon = 1e-05


def kernel(dims, x_ref, w_ref, taps_ref, lags_ref, out_ref, xrecv, xfull, toep, wcol, rcol, banded, filt,
           scores, seeds, stage, transit, final, own, ownrecv, xsem, dsend, fsend, srecv, tsend, trecv, frecv,
           osem):
    n_run, n_blk, frames, panel, fp, n_filter = dims
    half = panel // 2
    groups = half // 128
    total_frames = 2 * frames
    seeds_core = SEED_DEV // 2
    q_run = SEED_DEV // n_run
    rows_run = q_run * n_blk
    rows = rows_run // 2
    runs_core = n_run // 2

    z = lax.axis_index("run")
    tm = lax.axis_index("tm")
    blk = lax.axis_index("blk")
    other = 1 - tm

    def dev(run, core, block):
        return (run, core, block)

    barrier = pltpu.get_barrier_semaphore()
    mesh_id = pl.DeviceIdType.MESH
    pl.semaphore_signal(barrier, inc=1, device_id=dev(z, other, blk), device_id_type=mesh_id)
    for d in range(1, n_blk):
        peer = lax.rem(blk + d, n_blk)
        pl.semaphore_signal(barrier, inc=1, device_id=dev(z, tm, peer), device_id_type=mesh_id)

    @pl.when(z > 0)
    def _():
        for core in range(2):
            pl.semaphore_signal(barrier, inc=1, device_id=dev(z - 1, core, blk), device_id_type=mesh_id)

    @pl.when(z < n_run - 1)
    def _():
        for core in range(2):
            pl.semaphore_signal(barrier, inc=1, device_id=dev(z + 1, core, blk), device_id_type=mesh_id)

    inner = jnp.logical_and(z > 0, z < n_run - 1)
    pl.semaphore_wait(barrier, jnp.where(inner, n_blk + 4, n_blk + 2))

    mine = pl.ds(pl.multiple_of(tm * half, 128), half)
    theirs = pl.ds(pl.multiple_of(other * half, 128), half)
    swap = pltpu.make_async_remote_copy(
        src_ref=x_ref.at[:, theirs], dst_ref=xrecv, send_sem=xsem.at[0], recv_sem=xsem.at[1],
        device_id=dev(z, other, blk), device_id_type=mesh_id)
    swap.start()

    diff = (lax.broadcasted_iota(jnp.int32, (OUT_BLK, IN_BLK), 1)
            - lax.broadcasted_iota(jnp.int32, (OUT_BLK, IN_BLK), 0))
    band = jnp.zeros((OUT_BLK, IN_BLK), jnp.float32)
    for k in range(TAPS):
        band = jnp.where(diff == k, taps_ref[k], band)
    toep[...] = band.astype(jnp.bfloat16)

    wrow = w_ref[...].astype(jnp.float32)
    total = jnp.sum(wrow)
    wrow = jnp.concatenate([wrow, jnp.zeros((1, fp - total_frames), jnp.float32)], axis=1)
    for j in range(fp // 128):
        square = jnp.broadcast_to(wrow[:, j * 128:(j + 1) * 128], (128, 128)).T
        wcol[j * 128:(j + 1) * 128, :] = square
        rcol[j * 128:(j + 1) * 128, :] = jnp.sqrt(square)

    xfull[0:HALF, :] = jnp.zeros((HALF, half), jnp.float32)
    tail = HALF + total_frames
    xfull[tail:, :] = jnp.zeros((xfull.shape[0] - tail, half), jnp.float32)
    xfull[pl.ds(pl.multiple_of(HALF + tm * frames, 8), frames), :] = x_ref[:, mine].astype(jnp.float32)
    swap.wait_recv()
    xfull[pl.ds(pl.multiple_of(HALF + other * frames, 8), frames), :] = xrecv[...].astype(jnp.float32)

    for b in range(n_filter):
        banded[b * OUT_BLK:(b + 1) * OUT_BLK, :] = jnp.dot(
            toep[...], xfull[b * OUT_BLK:b * OUT_BLK + IN_BLK, :].astype(jnp.bfloat16),
            preferred_element_type=jnp.float32)

    lag_own = lags_ref[:, mine]
    for j in range(groups):
        lanes = slice(j * 128, (j + 1) * 128)
        lag = jnp.broadcast_to(lag_own[:, lanes], (CHUNK, 128))
        is_lag = [lag == v for v in range(LAGS)]

        def moments(i, carry, lanes=lanes, is_lag=is_lag):
            a1, a2 = carry
            r0 = pl.multiple_of(i * CHUNK, CHUNK)
            late = banded[pl.ds(r0, CHUNK + 8), lanes]
            v = late[0:CHUNK]
            for k in range(1, LAGS):
                v = jnp.where(is_lag[k], late[k:k + CHUNK], v)
            v = v.astype(jnp.bfloat16).astype(jnp.float32)
            filt[pl.ds(r0, CHUNK), lanes] = v
            wv = wcol[pl.ds(r0, CHUNK), :] * v
            a1 = a1 + jnp.sum(wv.reshape(CHUNK // 8, 8, 128), axis=0)
            a2 = a2 + jnp.sum((wv * v).reshape(CHUNK // 8, 8, 128), axis=0)
            return a1, a2

        zero = jnp.zeros((8, 128), jnp.float32)
        a1, a2 = lax.fori_loop(0, fp // CHUNK, moments, (zero, zero))
        first = jnp.sum(a1, axis=0, keepdims=True) / total
        second = jnp.sum(a2, axis=0, keepdims=True) / total
        scaling = lax.rsqrt(second - first * first + epsilon)

        def score(i, carry, lanes=lanes, first=first, scaling=scaling):
            r0 = pl.multiple_of(i * CHUNK, CHUNK)
            v = filt[pl.ds(r0, CHUNK), lanes]
            s = rcol[pl.ds(r0, CHUNK), :] * (v - first) * scaling
            scores[pl.ds(r0, CHUNK), lanes] = s.astype(jnp.bfloat16)
            return carry

        lax.fori_loop(0, fp // CHUNK, score, 0)

    pick = (lax.broadcasted_iota(jnp.int32, (seeds_core, half), 1)
            == (panel // SEED_DEV) * lax.broadcasted_iota(jnp.int32, (seeds_core, half), 0))
    seeds[blk, tm] = lax.dot_general(
        pick.astype(jnp.float32).astype(jnp.bfloat16), scores[...], (((1,), (1,)), ((), ())),
        preferred_element_type=jnp.float32).astype(jnp.bfloat16)

    def seed_copy(block, target, send):
        return pltpu.make_async_remote_copy(
            src_ref=seeds.at[block, tm], dst_ref=seeds.at[block, tm], send_sem=send,
            recv_sem=srecv.at[block, tm], device_id=target, device_id_type=mesh_id)

    for d in range(1, n_blk):
        peer = lax.rem(blk + d, n_blk)
        seed_copy(blk, dev(z, tm, peer), dsend.at[d]).start()
    seed_copy(blk, dev(z, other, blk), fsend.at[0]).start()
    for d in range(1, n_blk):
        peer = lax.rem(blk + n_blk - d, n_blk)
        pltpu.make_async_copy(seeds.at[peer, tm], seeds.at[peer, tm], srecv.at[peer, tm]).wait()
        seed_copy(peer, dev(z, other, blk), fsend.at[d]).start()
    for b in range(n_blk):
        pltpu.make_async_copy(seeds.at[b, other], seeds.at[b, other], srecv.at[b, other]).wait()

    i = lax.broadcasted_iota(jnp.int32, (rows_run, rows_run), 0)
    j = lax.broadcasted_iota(jnp.int32, (rows_run, rows_run), 1)
    n_vec = jnp.full((rows_run, rows_run), n_blk, jnp.int32)
    order = (j == lax.rem(i, n_vec) * q_run + lax.div(i, n_vec)).astype(jnp.float32).astype(jnp.bfloat16)

    def corr(r):
        core = lax.div(r, runs_core)
        q0 = pl.multiple_of(lax.rem(r, runs_core) * q_run, q_run)
        left = jnp.concatenate([seeds[b, core, pl.ds(q0, q_run), :] for b in range(n_blk)], axis=0)
        left = jnp.dot(order, left, preferred_element_type=jnp.float32).astype(jnp.bfloat16)
        return jnp.dot(left, scores[...], preferred_element_type=jnp.float32) / total

    code_row = groups * rows

    def encode(buf, v):
        peak = jnp.max(jnp.abs(v), axis=0, keepdims=True)
        lane = peak[:, 0:128]
        for g in range(1, groups):
            lane = jnp.maximum(lane, peak[:, g * 128:(g + 1) * 128])
        code = jnp.ceil(jnp.log2(jnp.maximum(lane, 1e-30)) * STEPS) + 1.0
        gain = TOP * jnp.exp2(code * (-1.0 / STEPS))
        for g in range(groups):
            scaled = jnp.round(v[:, g * 128:(g + 1) * 128] * gain)
            buf[g * rows:(g + 1) * rows, :] = scaled.astype(jnp.int32).astype(jnp.int16)
        buf[code_row:code_row + 16, :] = jnp.broadcast_to(code, (16, 128)).astype(jnp.int32).astype(jnp.int16)

    def decode(buf):
        code = buf[code_row:code_row + 16, :].astype(jnp.int32).astype(jnp.float32)[0:1, :]
        unit = jnp.exp2(code * (1.0 / STEPS)) * (1.0 / TOP)
        return jnp.concatenate(
            [buf[g * rows:(g + 1) * rows, :].astype(jnp.int32).astype(jnp.float32) * unit for g in range(groups)],
            axis=1)

    flip = (z >= runs_core).astype(jnp.int32)
    zz = z + flip * (n_run - 1 - 2 * z)

    def send_block(r, way, has_before):
        g = corr(r)
        nxt = z + 1 - 2 * way
        for h in range(2):
            own[h * rows:(h + 1) * rows, :] = g[h * rows:(h + 1) * rows, :]
        for h in range(2):

            @pl.when(has_before)
            def _():
                pltpu.make_async_copy(transit.at[r, h], transit.at[r, h], trecv.at[r, h]).wait()
                own[h * rows:(h + 1) * rows, :] += decode(transit.at[r, h])

            encode(stage.at[r, h], own[h * rows:(h + 1) * rows, :])

            @pl.when(r == nxt)
            def _():
                pltpu.make_async_remote_copy(
                    src_ref=stage.at[r, h], dst_ref=final.at[way, tm], send_sem=tsend.at[r, h],
                    recv_sem=frecv.at[way, tm], device_id=dev(nxt, h, blk), device_id_type=mesh_id).start()

            @pl.when(r != nxt)
            def _():
                pltpu.make_async_remote_copy(
                    src_ref=stage.at[r, h], dst_ref=transit.at[r, h], send_sem=tsend.at[r, h],
                    recv_sem=trecv.at[r, h], device_id=dev(nxt, tm, blk), device_id_type=mesh_id).start()

    def unflip(rr):
        return rr + flip * (n_run - 1 - 2 * rr)

    def step(k, carry):
        far = n_run - 1 - k

        @pl.when(far > zz)
        def _():
            send_block(unflip(far), flip, zz > 0)

        @pl.when(k < zz)
        def _():
            send_block(unflip(k), 1 - flip, zz < n_run - 1)

        return carry

    lax.fori_loop(0, n_run, step, 0)

    g = corr(z)
    own[...] = g
    keep = pl.ds(pl.multiple_of(tm * rows, rows), rows)
    give = pl.ds(pl.multiple_of(other * rows, rows), rows)
    trade = pltpu.make_async_remote_copy(
        src_ref=own.at[give, :], dst_ref=ownrecv, send_sem=osem.at[0], recv_sem=osem.at[1],
        device_id=dev(z, other, blk), device_id_type=mesh_id)
    trade.start()
    out_ref[:, mine] = own[keep, :]
    trade.wait_recv()
    out_ref[:, theirs] = ownrecv[...]
    for way, present in ((0, z > 0), (1, z < n_run - 1)):

        @pl.when(present)
        def _():
            for c in range(2):
                pltpu.make_async_copy(final.at[way, c], final.at[way, c], frecv.at[way, c]).wait()
                cols = slice(c * half, (c + 1) * half)
                out_ref[:, cols] += decode(final.at[way, c])

    out_ref[...] = out_ref[...] / n_run

    swap.wait_send()
    trade.wait_send()
    for d in range(n_blk):
        if d:
            seed_copy(blk, dev(z, tm, lax.rem(blk + d, n_blk)), dsend.at[d]).wait_send()
        seed_copy(blk, dev(z, other, blk), fsend.at[d]).wait_send()

    def drain(r, carry):
        @pl.when(r != z)
        def _():
            for h in range(2):
                pltpu.make_async_remote_copy(
                    src_ref=stage.at[r, h], dst_ref=transit.at[r, h], send_sem=tsend.at[r, h],
                    recv_sem=trecv.at[r, h], device_id=dev(z, other, blk), device_id_type=mesh_id).wait_send()

        return carry

    lax.fori_loop(0, n_run, drain, 0)


def local(n_run, n_blk, series, weights, taps, lags):
    signal = series[0]
    frames, panel = signal.shape
    half = panel // 2
    fp = -(-2 * frames // 256) * 256
    n_filter = -(-(fp + LAGS) // OUT_BLK)
    rows_run = SEED_DEV // n_run * n_blk
    rows = rows_run // 2
    message = (half // 128) * rows + 16
    vmem = pl.BlockSpec(memory_space=pltpu.VMEM)
    dma = pltpu.SemaphoreType.DMA
    f32, b16 = jnp.float32, jnp.bfloat16
    flops = 2 * half * fp * (IN_BLK + n_blk * SEED_DEV)
    return pl.pallas_call(
        functools.partial(kernel, (n_run, n_blk, frames, panel, fp, n_filter)),
        out_shape=jax.ShapeDtypeStruct((rows, panel), f32),
        in_specs=[vmem, vmem, pl.BlockSpec(memory_space=pltpu.SMEM), vmem],
        out_specs=vmem,
        scratch_shapes=[
            pltpu.VMEM((frames, half), b16),
            pltpu.VMEM((n_filter * OUT_BLK + IN_BLK - OUT_BLK, half), f32),
            pltpu.VMEM((OUT_BLK, IN_BLK), b16),
            pltpu.VMEM((fp, 128), f32),
            pltpu.VMEM((fp, 128), f32),
            pltpu.VMEM((n_filter * OUT_BLK, half), f32),
            pltpu.VMEM((fp, half), f32),
            pltpu.VMEM((fp, half), b16),
            pltpu.VMEM((n_blk, 2, SEED_DEV // 2, fp), b16),
            pltpu.VMEM((n_run, 2, message, 128), jnp.int16),
            pltpu.VMEM((n_run, 2, message, 128), jnp.int16),
            pltpu.VMEM((2, 2, message, 128), jnp.int16),
            pltpu.VMEM((rows_run, half), f32),
            pltpu.VMEM((rows, half), f32),
            dma((2,)),
            dma((n_blk,)),
            dma((n_blk,)),
            dma((n_blk, 2)),
            dma((n_run, 2)),
            dma((n_run, 2)),
            dma((2, 2)),
            dma((2,)),
        ],
        compiler_params=pltpu.CompilerParams(
            collective_id=0, has_side_effects=True, vmem_limit_bytes=56 * 1024 * 1024),
        cost_estimate=pl.CostEstimate(flops=flops, bytes_accessed=2 * frames * panel, transcendentals=0),
    )(signal, weights, taps.astype(f32), lags[None, :])


def solution(mesh):
    placed = (P("run", "tm", "blk"), P("run", None), P(), P("blk"))
    body = functools.partial(local, mesh.shape["run"], mesh.shape["blk"])
    return jax.shard_map(
        body, mesh=mesh, in_specs=placed, out_specs=P(("run", "tm"), "blk"), check_vma=False
    )
```

time: 179 us -> 45.9 us (0.26)
  the two profiles are of different devices: /device:TPU:0 before, /device:TPU:19 now
where the time goes in v1:
time: 45.9 us; the launch traced here: 45.1 us
  Pallas kernels  40.8 us (89%)
  local copies, waits for them, and re-layouts  3.06 us (7%)
  other arithmetic  1.23 us (3%)
    pallas_call x1, Pallas kernels, local(): pl.pallas_call(functools.partial(kernel, (n_run, n_blk, frames, panel, fp...  40.8 us
    unnamed x1, local copies, waits for them, and re-layouts  1.77 us
    broadcast_in_dim x1, local copies, waits for them, and re-layouts, local(): lags[None, :]  1.29 us
    convert_element_type x1, other arithmetic, local(): taps.astype(f32)  1.23 us

profile of v1, /device:TPU:19, one launch (start us, length us, event | category | flops | bytes accessed | tf_op | source)
XLA Modules:
  0.0 45.1 jit_solution(6164200643317476231)
XLA Ops:
  0.0 1.2 %convert_element_type.3.taps_ref = f32[33]{0:T(128)} convert(bf16[33]{0:T(256)(128)(2,1)} %param.6) | non-fusion elementwise | flops 33 | bytes 198 | tf_op jit(solution)/shard_map/convert_element_type | solution.py:321
  1.2 1.3 %broadcast_in_dim.3.lags_ref = s32[1,1536]{1,0:T(1,128)} reshape(s32[1536]{0:T(1024)} %param.7) | data formatting | bytes 12288 | tf_op jit(solution)/shard_map/broadcast_in_dim | solution.py:321
  2.5 40.8 %shard_map.46 = f32[64,1536]{1,0:T(8,128)} custom-call(bf16[600,1536]{1,0:T(8,128)(2,1)} %bitcast.1, s32[1,1200]{1,0:T(1,128)} %w_ref.1, f32[33]{0:T(128)} %convert_element_type.3.taps_ref, s32[1,1536]{1,0:T(1,128)} %broadcast_in_dim.3.lags_ref), custom_call_target="tpu_custom_call" | custom-call | flops 1509949440 | bytes 1843200 | tf_op jit(solution)/shard_map/pallas_call | solution.py:289
  43.3 1.8 %copy.6 = f32[64,1536]{1,0:T(8,128)} copy(f32[64,1536]{1,0:T(8,128)} %shard_map.46) | data formatting | bytes 786432

commit v2 on v1

v2 whole, which is shorter than its diff:
```python
import functools

import jax
import jax.numpy as jnp
from jax import lax
from jax.experimental import pallas as pl
from jax.experimental.pallas import tpu as pltpu
from jax.sharding import PartitionSpec as P

HALF = 16
LAGS = 4
SEED_DEV = 128
TAPS = 2 * HALF + 1
OUT_BLK = 224
IN_BLK = 256
CHUNK = 128
TOP = 32000.0
STEPS = 128.0
epsilon = 1e-05


def kernel(dims, x_ref, w_ref, taps_ref, lags_ref, out_ref, sown, sother, sfull, sscore, xrecv, xfull, toep, wcol,
           rcol, lagscr, banded, filt, scores, seeds, stage, transit, final, own, ownrecv, xsem, dsend, srecv, tsend,
           trecv, frecv, osem):
    n_run, n_blk, frames, panel, fp, n_filter = dims
    half = panel // 2
    groups = half // 128
    total_frames = 2 * frames
    q_run = SEED_DEV // n_run
    rows_run = q_run * n_blk
    rows = rows_run // 2
    runs_core = n_run // 2

    z = lax.axis_index("run")
    tm = lax.axis_index("tm")
    blk = lax.axis_index("blk")
    other = 1 - tm

    def dev(run, core, block):
        return (run, core, block)

    barrier = pltpu.get_barrier_semaphore()
    mesh_id = pl.DeviceIdType.MESH
    pl.semaphore_signal(barrier, inc=1, device_id=dev(z, other, blk), device_id_type=mesh_id)
    for d in range(1, n_blk):
        peer = lax.rem(blk + d, n_blk)
        pl.semaphore_signal(barrier, inc=1, device_id=dev(z, tm, peer), device_id_type=mesh_id)

    @pl.when(z > 0)
    def _():
        for core in range(2):
            pl.semaphore_signal(barrier, inc=1, device_id=dev(z - 1, core, blk), device_id_type=mesh_id)

    @pl.when(z < n_run - 1)
    def _():
        for core in range(2):
            pl.semaphore_signal(barrier, inc=1, device_id=dev(z + 1, core, blk), device_id_type=mesh_id)

    def one_hot(mask):
        return mask.astype(jnp.float32).astype(jnp.bfloat16)

    pick = one_hot(lax.broadcasted_iota(jnp.int32, (panel, SEED_DEV), 0)
                   == (panel // SEED_DEV) * lax.broadcasted_iota(jnp.int32, (panel, SEED_DEV), 1))
    sown[...] = jnp.dot(x_ref[...], pick, preferred_element_type=jnp.float32).astype(jnp.bfloat16)

    inner = jnp.logical_and(z > 0, z < n_run - 1)
    pl.semaphore_wait(barrier, jnp.where(inner, n_blk + 4, n_blk + 2))

    mine = pl.ds(pl.multiple_of(tm * half, 128), half)
    theirs = pl.ds(pl.multiple_of(other * half, 128), half)
    sswap = pltpu.make_async_remote_copy(
        src_ref=sown, dst_ref=sother, send_sem=xsem.at[2], recv_sem=xsem.at[3],
        device_id=dev(z, other, blk), device_id_type=mesh_id)
    sswap.start()
    swap = pltpu.make_async_remote_copy(
        src_ref=x_ref.at[:, theirs], dst_ref=xrecv, send_sem=xsem.at[0], recv_sem=xsem.at[1],
        device_id=dev(z, other, blk), device_id_type=mesh_id)
    swap.start()

    diff = (lax.broadcasted_iota(jnp.int32, (OUT_BLK, IN_BLK), 1)
            - lax.broadcasted_iota(jnp.int32, (OUT_BLK, IN_BLK), 0))
    band = jnp.zeros((OUT_BLK, IN_BLK), jnp.float32)
    for k in range(TAPS):
        band = jnp.where(diff == k, taps_ref[k], band)
    toep[...] = band.astype(jnp.bfloat16)

    wrow = w_ref[...].astype(jnp.float32)
    total = jnp.sum(wrow)
    wrow = jnp.concatenate([wrow, jnp.zeros((1, fp - total_frames), jnp.float32)], axis=1)
    for j in range(fp // 128):
        square = jnp.broadcast_to(wrow[:, j * 128:(j + 1) * 128], (128, 128)).T
        wcol[j * 128:(j + 1) * 128, :] = square
        rcol[j * 128:(j + 1) * 128, :] = jnp.sqrt(square)

    tail = HALF + total_frames
    near = pl.ds(pl.multiple_of(HALF + tm * frames, 8), frames)
    far_rows = pl.ds(pl.multiple_of(HALF + other * frames, 8), frames)

    def edges(ref, width):
        ref[0:HALF, :] = jnp.zeros((HALF, width), jnp.float32)
        ref[tail:, :] = jnp.zeros((ref.shape[0] - tail, width), jnp.float32)

    def normalize(src, lanes, lag, dst):
        width = lag.shape[1]
        for b in range(n_filter):
            banded[b * OUT_BLK:(b + 1) * OUT_BLK, 0:width] = jnp.dot(
                toep[...], src[b * OUT_BLK:b * OUT_BLK + IN_BLK, lanes].astype(jnp.bfloat16),
                preferred_element_type=jnp.float32)
        for g in range(width // 128):
            part = slice(g * 128, (g + 1) * 128)
            odd = jnp.broadcast_to((lag[:, part] & 1) == 1, (CHUNK + 8, 128))
            high = jnp.broadcast_to(lag[:, part] >= 2, (CHUNK, 128))
            sums = []
            for r0 in range(0, fp, CHUNK):
                late = banded[r0:r0 + CHUNK + 16, part]
                v = jnp.where(odd, late[1:CHUNK + 9], late[0:CHUNK + 8])
                v = jnp.where(high, v[2:CHUNK + 2], v[0:CHUNK])
                v = v.astype(jnp.bfloat16).astype(jnp.float32)
                filt[r0:r0 + CHUNK, part] = v
                wv = wcol[r0:r0 + CHUNK, :] * v
                sums.append((jnp.sum(wv.reshape(CHUNK // 8, 8, 128), axis=0),
                             jnp.sum((wv * v).reshape(CHUNK // 8, 8, 128), axis=0)))
            first = jnp.sum(sum(a for a, _ in sums), axis=0, keepdims=True) / total
            second = jnp.sum(sum(a for _, a in sums), axis=0, keepdims=True) / total
            scaling = lax.rsqrt(second - first * first + epsilon)
            for r0 in range(0, fp, CHUNK):
                v = rcol[r0:r0 + CHUNK, :] * (filt[r0:r0 + CHUNK, part] - first) * scaling
                dst(r0, g, v.astype(jnp.bfloat16))

    edges(sfull, SEED_DEV)
    sfull[near, :] = sown[...].astype(jnp.float32)
    lag_rows = [lags_ref[j:j + 1, :] for j in range(panel // 128)]
    lag_all = jnp.broadcast_to(jnp.concatenate(lag_rows, axis=1), (8, panel)).astype(jnp.float32)
    seed_lag = jnp.dot(lag_all.astype(jnp.bfloat16), pick, preferred_element_type=jnp.float32)
    seed_lag = seed_lag.astype(jnp.int32)[0:1, :]
    sswap.wait_recv()
    sfull[far_rows, :] = sother[...].astype(jnp.float32)

    def seed_store(r0, g, v):
        sscore[r0:r0 + CHUNK, :] = v

    normalize(sfull, slice(0, SEED_DEV), seed_lag, seed_store)
    eye = one_hot(lax.broadcasted_iota(jnp.int32, (SEED_DEV, SEED_DEV), 1)
                  == lax.broadcasted_iota(jnp.int32, (SEED_DEV, SEED_DEV), 0))
    rows_seed = lax.dot_general(
        eye, sscore[...], (((1,), (1,)), ((), ())), preferred_element_type=jnp.float32).astype(jnp.bfloat16)
    for r in range(n_run):
        seeds[blk, r] = rows_seed[r * q_run:(r + 1) * q_run, :]

    flip = (z >= runs_core).astype(jnp.int32)
    zz = z + flip * (n_run - 1 - 2 * z)

    def unflip(rr):
        return rr + flip * (n_run - 1 - 2 * rr)

    def in_order(away, back):
        def step(k, carry):
            far = n_run - 1 - k

            @pl.when(far > zz)
            def _():
                away(unflip(far))

            @pl.when(k < zz)
            def _():
                back(unflip(k))

            return carry

        lax.fori_loop(0, n_run, step, 0)

    def seed_copy(d, r):
        return pltpu.make_async_remote_copy(
            src_ref=seeds.at[blk, r], dst_ref=seeds.at[blk, r], send_sem=dsend.at[d, r],
            recv_sem=srecv.at[blk, r], device_id=dev(z, tm, lax.rem(blk + d, n_blk)), device_id_type=mesh_id)

    def send_seeds(r):
        for d in range(1, n_blk):
            seed_copy(d, r).start()

    in_order(send_seeds, send_seeds)
    send_seeds(z)

    edges(xfull, half)
    xfull[near, :] = x_ref[:, mine].astype(jnp.float32)
    swap.wait_recv()
    xfull[far_rows, :] = xrecv[...].astype(jnp.float32)
    lag_own = jnp.where(tm == 0, jnp.concatenate(lag_rows[:groups], axis=1),
                        jnp.concatenate(lag_rows[groups:], axis=1))
    for g in range(groups):
        lagscr[g:g + 1, :] = lag_own[:, g * 128:(g + 1) * 128]

    def pair(p, carry):
        lane0 = pl.multiple_of(p * 256, 256)
        lag = jnp.concatenate([lagscr[pl.ds(2 * p, 1), :], lagscr[pl.ds(2 * p + 1, 1), :]], axis=1)

        def store(r0, g, v):
            scores[r0:r0 + CHUNK, pl.ds(pl.multiple_of(lane0 + g * 128, 128), 128)] = v

        normalize(xfull, pl.ds(lane0, 256), lag, store)
        return carry

    lax.fori_loop(0, half // 256, pair, 0)

    i = lax.broadcasted_iota(jnp.int32, (rows_run, rows_run), 0)
    j = lax.broadcasted_iota(jnp.int32, (rows_run, rows_run), 1)
    n_vec = jnp.full((rows_run, rows_run), n_blk, jnp.int32)
    order = one_hot(j == lax.rem(i, n_vec) * q_run + lax.div(i, n_vec))

    def corr(r):
        for d in range(1, n_blk):
            peer = lax.rem(blk + d, n_blk)
            pltpu.make_async_copy(seeds.at[peer, r], seeds.at[peer, r], srecv.at[peer, r]).wait()
        left = jnp.concatenate([seeds[b, r] for b in range(n_blk)], axis=0)
        left = jnp.dot(order, left, preferred_element_type=jnp.float32).astype(jnp.bfloat16)
        return jnp.dot(left, scores[...], preferred_element_type=jnp.float32) / total

    code_row = groups * rows

    def encode(buf, v):
        peak = jnp.max(jnp.abs(v), axis=0, keepdims=True)
        lane = peak[:, 0:128]
        for g in range(1, groups):
            lane = jnp.maximum(lane, peak[:, g * 128:(g + 1) * 128])
        code = jnp.ceil(jnp.log2(jnp.maximum(lane, 1e-30)) * STEPS) + 1.0
        gain = TOP * jnp.exp2(code * (-1.0 / STEPS))
        for g in range(groups):
            scaled = jnp.round(v[:, g * 128:(g + 1) * 128] * gain)
            buf[g * rows:(g + 1) * rows, :] = scaled.astype(jnp.int32).astype(jnp.int16)
        buf[code_row:code_row + 16, :] = jnp.broadcast_to(code, (16, 128)).astype(jnp.int32).astype(jnp.int16)

    def decode(buf):
        code = buf[code_row:code_row + 16, :].astype(jnp.int32).astype(jnp.float32)[0:1, :]
        unit = jnp.exp2(code * (1.0 / STEPS)) * (1.0 / TOP)
        return jnp.concatenate(
            [buf[g * rows:(g + 1) * rows, :].astype(jnp.int32).astype(jnp.float32) * unit for g in range(groups)],
            axis=1)

    def send_block(r, way, has_before):
        g = corr(r)
        nxt = z + 1 - 2 * way
        for h in range(2):
            own[h * rows:(h + 1) * rows, :] = g[h * rows:(h + 1) * rows, :]
        for h in range(2):

            @pl.when(has_before)
            def _():
                pltpu.make_async_copy(transit.at[r, h], transit.at[r, h], trecv.at[r, h]).wait()
                own[h * rows:(h + 1) * rows, :] += decode(transit.at[r, h])

            encode(stage.at[r, h], own[h * rows:(h + 1) * rows, :])

            @pl.when(r == nxt)
            def _():
                pltpu.make_async_remote_copy(
                    src_ref=stage.at[r, h], dst_ref=final.at[way, tm], send_sem=tsend.at[r, h],
                    recv_sem=frecv.at[way, tm], device_id=dev(nxt, h, blk), device_id_type=mesh_id).start()

            @pl.when(r != nxt)
            def _():
                pltpu.make_async_remote_copy(
                    src_ref=stage.at[r, h], dst_ref=transit.at[r, h], send_sem=tsend.at[r, h],
                    recv_sem=trecv.at[r, h], device_id=dev(nxt, tm, blk), device_id_type=mesh_id).start()

    in_order(lambda r: send_block(r, flip, zz > 0), lambda r: send_block(r, 1 - flip, zz < n_run - 1))

    g = corr(z)
    own[...] = g
    keep = pl.ds(pl.multiple_of(tm * rows, rows), rows)
    give = pl.ds(pl.multiple_of(other * rows, rows), rows)
    trade = pltpu.make_async_remote_copy(
        src_ref=own.at[give, :], dst_ref=ownrecv, send_sem=osem.at[0], recv_sem=osem.at[1],
        device_id=dev(z, other, blk), device_id_type=mesh_id)
    trade.start()
    out_ref[:, mine] = own[keep, :]
    trade.wait_recv()
    out_ref[:, theirs] = ownrecv[...]
    for way, present in ((0, z > 0), (1, z < n_run - 1)):

        @pl.when(present)
        def _():
            for c in range(2):
                pltpu.make_async_copy(final.at[way, c], final.at[way, c], frecv.at[way, c]).wait()
                cols = slice(c * half, (c + 1) * half)
                out_ref[:, cols] += decode(final.at[way, c])

    out_ref[...] = out_ref[...] / n_run

    sswap.wait_send()
    swap.wait_send()
    trade.wait_send()

    def drain(r, carry):
        for d in range(1, n_blk):
            seed_copy(d, r).wait_send()

        @pl.when(r != z)
        def _():
            for h in range(2):
                pltpu.make_async_remote_copy(
                    src_ref=stage.at[r, h], dst_ref=transit.at[r, h], send_sem=tsend.at[r, h],
                    recv_sem=trecv.at[r, h], device_id=dev(z, other, blk), device_id_type=mesh_id).wait_send()

        return carry

    lax.fori_loop(0, n_run, drain, 0)


def local(n_run, n_blk, series, weights, taps, lags):
    signal = series[0]
    frames, panel = signal.shape
    half = panel // 2
    fp = -(-2 * frames // 256) * 256
    n_filter = -(-(fp + LAGS) // OUT_BLK)
    rows_run = SEED_DEV // n_run * n_blk
    rows = rows_run // 2
    message = (half // 128) * rows + 16
    vmem = pl.BlockSpec(memory_space=pltpu.VMEM)
    dma = pltpu.SemaphoreType.DMA
    f32, b16 = jnp.float32, jnp.bfloat16
    flops = 2 * half * fp * (IN_BLK + n_blk * SEED_DEV)
    return pl.pallas_call(
        functools.partial(kernel, (n_run, n_blk, frames, panel, fp, n_filter)),
        out_shape=jax.ShapeDtypeStruct((rows, panel), f32),
        in_specs=[vmem, vmem, pl.BlockSpec(memory_space=pltpu.SMEM), vmem],
        out_specs=vmem,
        scratch_shapes=[
            pltpu.VMEM((frames, SEED_DEV), b16),
            pltpu.VMEM((frames, SEED_DEV), b16),
            pltpu.VMEM((n_filter * OUT_BLK + IN_BLK - OUT_BLK, SEED_DEV), f32),
            pltpu.VMEM((fp, SEED_DEV), b16),
            pltpu.VMEM((frames, half), b16),
            pltpu.VMEM((n_filter * OUT_BLK + IN_BLK - OUT_BLK, half), f32),
            pltpu.VMEM((OUT_BLK, IN_BLK), b16),
            pltpu.VMEM((fp, 128), f32),
            pltpu.VMEM((fp, 128), f32),
            pltpu.VMEM((half // 128, 128), jnp.int32),
            pltpu.VMEM((n_filter * OUT_BLK, 256), f32),
            pltpu.VMEM((fp, 256), f32),
            pltpu.VMEM((fp, half), b16),
            pltpu.VMEM((n_blk, n_run, SEED_DEV // n_run, fp), b16),
            pltpu.VMEM((n_run, 2, message, 128), jnp.int16),
            pltpu.VMEM((n_run, 2, message, 128), jnp.int16),
            pltpu.VMEM((2, 2, message, 128), jnp.int16),
            pltpu.VMEM((rows_run, half), f32),
            pltpu.VMEM((rows, half), f32),
            dma((4,)),
            dma((n_blk, n_run)),
            dma((n_blk, n_run)),
            dma((n_run, 2)),
            dma((n_run, 2)),
            dma((2, 2)),
            dma((2,)),
        ],
        compiler_params=pltpu.CompilerParams(
            collective_id=0, has_side_effects=True, vmem_limit_bytes=56 * 1024 * 1024),
        cost_estimate=pl.CostEstimate(flops=flops, bytes_accessed=2 * frames * panel, transcendentals=0),
    )(signal, weights, taps.astype(f32), lags.reshape(panel // 128, 128))


def solution(mesh):
    placed = (P("run", "tm", "blk"), P("run", None), P(), P("blk"))
    body = functools.partial(local, mesh.shape["run"], mesh.shape["blk"])
    return jax.shard_map(
        body, mesh=mesh, in_specs=placed, out_specs=P(("run", "tm"), "blk"), check_vma=False
    )
```

time: 45.9 us -> 33.8 us (0.74); the launches traced: 45.1 us -> 33.6 us
  Pallas kernels: 40.8 us -> 30.6 us
  local copies, waits for them, and re-layouts: 3.06 us -> 1.77 us
    pallas_call x1, Pallas kernels: 40.8 us -> 30.6 us  [local(): pl.pallas_call(functools.partial(kernel, (n_run, n_blk, frames, panel, fp...]
    broadcast_in_dim x1 -> x0, local copies, waits for them, and re-layouts: 1.29 us -> none  [local(): lags[None, :]]
where the time goes in v2:
time: 33.8 us; the launch traced here: 33.6 us
  Pallas kernels  30.6 us (91%)
  local copies, waits for them, and re-layouts  1.77 us (5%)
  other arithmetic  1.17 us (3%)
    pallas_call x1, Pallas kernels, local(): pl.pallas_call(functools.partial(kernel, (n_run, n_blk, frames, panel, fp...  30.6 us
    unnamed x1, local copies, waits for them, and re-layouts  1.77 us
    convert_element_type x1, other arithmetic, local(): taps.astype(f32)  1.17 us

profile of v2, /device:TPU:19, one launch (start us, length us, event | category | flops | bytes accessed | tf_op | source)
XLA Modules:
  0.0 33.6 jit_solution(14760262912297556659)
XLA Ops:
  0.0 1.2 %convert_element_type.3.taps_ref = f32[33]{0:T(128)} convert(bf16[33]{0:T(256)(128)(2,1)} %param.6) | non-fusion elementwise | flops 33 | bytes 198 | tf_op jit(solution)/shard_map/convert_element_type | solution.py:358
  1.2 30.6 %shard_map.46 = f32[64,1536]{1,0:T(8,128)} custom-call(bf16[600,1536]{1,0:T(8,128)(2,1)} %bitcast.2, s32[1,1200]{1,0:T(1,128)} %w_ref.1, f32[33]{0:T(128)} %convert_element_type.3.taps_ref, s32[12,128]{1,0:T(8,128)} %bitcast.3), custom_call_target="tpu_custom_call" | custom-call | flops 1509949440 | bytes 1843200 | tf_op jit(solution)/shard_map/pallas_call | solution.py:322
  31.8 1.8 %copy.6 = f32[64,1536]{1,0:T(8,128)} copy(f32[64,1536]{1,0:T(8,128)} %shard_map.46) | data formatting | bytes 786432

commit v3 on v2

v3 whole, which is shorter than its diff:
```python
import functools

import jax
import jax.numpy as jnp
from jax import lax
from jax.experimental import pallas as pl
from jax.experimental.pallas import tpu as pltpu
from jax.sharding import PartitionSpec as P

HALF = 16
LAGS = 4
SEED_DEV = 128
TAPS = 2 * HALF + 1
OUT_BLK = 224
IN_BLK = 256
CHUNK = 128
WIDE = 256
TOP = 32000.0
STEPS = 128.0
epsilon = 1e-05


def kernel(dims, x_hbm, w_ref, taps_ref, lags_ref, out_ref, x_ref, sown, sother, sfull, sscore, xrecv, xfull, toep, wcol,
           rcol, lagscr, banded, filt, scores, seeds, left, stage, transit, final, part, own, ownrecv, xsem, dsend, srecv, tsend,
           trecv, frecv, osem):
    n_run, n_blk, frames, panel, fp, n_filter = dims
    half = panel // 2
    groups = half // 128
    total_frames = 2 * frames
    q_run = SEED_DEV // n_run
    rows_run = q_run * n_blk
    rows = rows_run // 2
    runs_core = n_run // 2

    z = lax.axis_index("run")
    tm = lax.axis_index("tm")
    blk = lax.axis_index("blk")
    other = 1 - tm

    def dev(run, core, block):
        return (run, core, block)

    barrier = pltpu.get_barrier_semaphore()
    mesh_id = pl.DeviceIdType.MESH
    pl.semaphore_signal(barrier, inc=1, device_id=dev(z, other, blk), device_id_type=mesh_id)
    for d in range(1, n_blk):
        peer = lax.rem(blk + d, n_blk)
        pl.semaphore_signal(barrier, inc=1, device_id=dev(z, tm, peer), device_id_type=mesh_id)

    @pl.when(z > 0)
    def _():
        for core in range(2):
            pl.semaphore_signal(barrier, inc=1, device_id=dev(z - 1, core, blk), device_id_type=mesh_id)

    @pl.when(z < n_run - 1)
    def _():
        for core in range(2):
            pl.semaphore_signal(barrier, inc=1, device_id=dev(z + 1, core, blk), device_id_type=mesh_id)

    mine = pl.ds(pl.multiple_of(tm * half, 128), half)
    theirs = pl.ds(pl.multiple_of(other * half, 128), half)
    load = pltpu.make_async_copy(x_hbm, x_ref, xsem.at[4])
    load.start()

    diff = (lax.broadcasted_iota(jnp.int32, (OUT_BLK, IN_BLK), 1)
            - lax.broadcasted_iota(jnp.int32, (OUT_BLK, IN_BLK), 0))
    band = jnp.zeros((OUT_BLK, IN_BLK), jnp.float32)
    for k in range(TAPS):
        band = jnp.where(diff == k, taps_ref[k].astype(jnp.float32), band)
    toep[...] = band.astype(jnp.bfloat16)

    wrow = w_ref[...].astype(jnp.float32)
    total = jnp.sum(wrow)
    wrow = jnp.concatenate([wrow, jnp.zeros((1, fp - total_frames), jnp.float32)], axis=1)
    for j in range(fp // 128):
        square = jnp.broadcast_to(wrow[:, j * 128:(j + 1) * 128], (128, 128)).T
        wcol[j * 128:(j + 1) * 128, :] = square
        rcol[j * 128:(j + 1) * 128, :] = jnp.sqrt(square)

    def one_hot(mask):
        return mask.astype(jnp.float32).astype(jnp.bfloat16)

    pick = one_hot(lax.broadcasted_iota(jnp.int32, (panel, SEED_DEV), 0)
                   == (panel // SEED_DEV) * lax.broadcasted_iota(jnp.int32, (panel, SEED_DEV), 1))
    load.wait()
    sown[...] = jnp.dot(x_ref[...], pick, preferred_element_type=jnp.float32).astype(jnp.bfloat16)

    inner = jnp.logical_and(z > 0, z < n_run - 1)
    pl.semaphore_wait(barrier, jnp.where(inner, n_blk + 4, n_blk + 2))

    sswap = pltpu.make_async_remote_copy(
        src_ref=sown, dst_ref=sother, send_sem=xsem.at[2], recv_sem=xsem.at[3],
        device_id=dev(z, other, blk), device_id_type=mesh_id)
    sswap.start()
    swap = pltpu.make_async_remote_copy(
        src_ref=x_ref.at[:, theirs], dst_ref=xrecv, send_sem=xsem.at[0], recv_sem=xsem.at[1],
        device_id=dev(z, other, blk), device_id_type=mesh_id)
    swap.start()

    tail = HALF + total_frames
    near = pl.ds(pl.multiple_of(HALF + tm * frames, 8), frames)
    far_rows = pl.ds(pl.multiple_of(HALF + other * frames, 8), frames)

    def edges(ref, width):
        ref[0:HALF, :] = jnp.zeros((HALF, width), jnp.float32)
        ref[tail:, :] = jnp.zeros((ref.shape[0] - tail, width), jnp.float32)

    def normalize(src, lanes, lag, dst):
        width = lag.shape[1]
        for b in range(n_filter):
            banded[b * OUT_BLK:(b + 1) * OUT_BLK, 0:width] = jnp.dot(
                toep[...], src[b * OUT_BLK:b * OUT_BLK + IN_BLK, lanes].astype(jnp.bfloat16),
                preferred_element_type=jnp.float32)
        for g in range(width // 128):
            part = slice(g * 128, (g + 1) * 128)
            odd = jnp.broadcast_to((lag[:, part] & 1) == 1, (CHUNK + 8, 128))
            high = jnp.broadcast_to(lag[:, part] >= 2, (CHUNK, 128))
            sums = []
            for r0 in range(0, fp, CHUNK):
                late = banded[r0:r0 + CHUNK + 16, part]
                v = jnp.where(odd, late[1:CHUNK + 9], late[0:CHUNK + 8])
                v = jnp.where(high, v[2:CHUNK + 2], v[0:CHUNK])
                v = v.astype(jnp.bfloat16).astype(jnp.float32)
                filt[r0:r0 + CHUNK, part] = v
                wv = wcol[r0:r0 + CHUNK, :] * v
                sums.append((jnp.sum(wv.reshape(CHUNK // 8, 8, 128), axis=0),
                             jnp.sum((wv * v).reshape(CHUNK // 8, 8, 128), axis=0)))
            first = jnp.sum(sum(a for a, _ in sums), axis=0, keepdims=True) / total
            second = jnp.sum(sum(a for _, a in sums), axis=0, keepdims=True) / total
            scaling = lax.rsqrt(second - first * first + epsilon)
            for r0 in range(0, fp, CHUNK):
                v = rcol[r0:r0 + CHUNK, :] * (filt[r0:r0 + CHUNK, part] - first) * scaling
                dst(r0, g, v.astype(jnp.bfloat16))

    edges(sfull, SEED_DEV)
    sfull[near, :] = sown[...].astype(jnp.float32)
    lag_rows = [lags_ref[j:j + 1, :] for j in range(panel // 128)]
    lag_all = jnp.broadcast_to(jnp.concatenate(lag_rows, axis=1), (8, panel)).astype(jnp.float32)
    seed_lag = jnp.dot(lag_all.astype(jnp.bfloat16), pick, preferred_element_type=jnp.float32)
    seed_lag = seed_lag.astype(jnp.int32)[0:1, :]
    edges(xfull, half)
    xfull[near, :] = x_ref[:, mine].astype(jnp.float32)
    sswap.wait_recv()
    sfull[far_rows, :] = sother[...].astype(jnp.float32)

    def seed_store(r0, g, v):
        sscore[r0:r0 + CHUNK, :] = v

    normalize(sfull, slice(0, SEED_DEV), seed_lag, seed_store)
    eye = one_hot(lax.broadcasted_iota(jnp.int32, (SEED_DEV, SEED_DEV), 1)
                  == lax.broadcasted_iota(jnp.int32, (SEED_DEV, SEED_DEV), 0))
    rows_seed = lax.dot_general(
        eye, sscore[...], (((1,), (1,)), ((), ())), preferred_element_type=jnp.float32).astype(jnp.bfloat16)
    for r in range(n_run):
        seeds[blk, r] = rows_seed[r * q_run:(r + 1) * q_run, :]

    flip = (z >= runs_core).astype(jnp.int32)
    zz = z + flip * (n_run - 1 - 2 * z)

    def unflip(rr):
        return rr + flip * (n_run - 1 - 2 * rr)

    def in_order(out, home, skip=False):
        def step(k, carry):
            far = n_run - 1 - k

            @pl.when(jnp.logical_and(far > zz, k > 0) if skip else far > zz)
            def _():
                out(unflip(far))

            @pl.when(k < zz)
            def _():
                home(unflip(k))

            return carry

        lax.fori_loop(0, n_run, step, 0)

    def seed_copy(d, r):
        return pltpu.make_async_remote_copy(
            src_ref=seeds.at[blk, r], dst_ref=seeds.at[blk, r], send_sem=dsend.at[d, r],
            recv_sem=srecv.at[blk, r], device_id=dev(z, tm, lax.rem(blk + d, n_blk)), device_id_type=mesh_id)

    def send_seeds(r):
        for d in range(1, n_blk):
            seed_copy(d, r).start()

    in_order(send_seeds, send_seeds)
    send_seeds(z)

    swap.wait_recv()
    xfull[far_rows, :] = xrecv[...].astype(jnp.float32)
    lag_own = jnp.where(tm == 0, jnp.concatenate(lag_rows[:groups], axis=1),
                        jnp.concatenate(lag_rows[groups:], axis=1))
    for g in range(groups):
        lagscr[g:g + 1, :] = lag_own[:, g * 128:(g + 1) * 128]

    i = lax.broadcasted_iota(jnp.int32, (rows_run, rows_run), 0)
    j = lax.broadcasted_iota(jnp.int32, (rows_run, rows_run), 1)
    n_vec = jnp.full((rows_run, rows_run), n_blk, jnp.int32)
    order = one_hot(j == lax.rem(i, n_vec) * q_run + lax.div(i, n_vec))

    def prepare(r):
        for d in range(1, n_blk):
            peer = lax.rem(blk + d, n_blk)
            pltpu.make_async_copy(seeds.at[peer, r], seeds.at[peer, r], srecv.at[peer, r]).wait()
        rows_left = jnp.concatenate([seeds[b, r] for b in range(n_blk)], axis=0)
        left[...] = jnp.dot(order, rows_left, preferred_element_type=jnp.float32).astype(jnp.bfloat16)

    def corr(p):
        cols = pl.ds(pl.multiple_of(p * WIDE, WIDE), WIDE)
        return jnp.dot(left[...], scores[:, cols], preferred_element_type=jnp.float32) / total

    def encode(buf, at, v):
        count = v.shape[0]
        peak = jnp.max(jnp.abs(v), axis=0, keepdims=True)
        lane = jnp.maximum(peak[:, 0:128], peak[:, 128:256])
        code = jnp.ceil(jnp.log2(jnp.maximum(lane, 1e-30)) * STEPS) + 1.0
        gain = TOP * jnp.exp2(code * (-1.0 / STEPS))
        for g in range(2):
            scaled = jnp.round(v[:, g * 128:(g + 1) * 128] * gain)
            buf[at + g * count:at + (g + 1) * count, :] = scaled.astype(jnp.int32).astype(jnp.int16)
        at += 2 * count
        buf[at:at + 16, :] = jnp.broadcast_to(code, (16, 128)).astype(jnp.int32).astype(jnp.int16)

    def decode(buf, count):
        code = buf[2 * count:2 * count + 16, :].astype(jnp.int32).astype(jnp.float32)[0:1, :]
        unit = jnp.exp2(code * (1.0 / STEPS)) * (1.0 / TOP)
        return jnp.concatenate(
            [buf[g * count:(g + 1) * count, :].astype(jnp.int32).astype(jnp.float32) * unit for g in range(2)],
            axis=1)

    long, short = 2 * rows_run + 16, 2 * rows + 16

    def pass_on(r, p):
        nxt = jnp.where(r > z, z + 1, z - 1)
        return pltpu.make_async_remote_copy(
            src_ref=stage.at[r, p, pl.ds(0, long)], dst_ref=transit.at[r, p], send_sem=tsend.at[r, p, 0],
            recv_sem=trecv.at[r, p], device_id=dev(nxt, tm, blk), device_id_type=mesh_id)

    def deliver(r, p, h):
        way = jnp.where(r > z, 0, 1)
        return pltpu.make_async_remote_copy(
            src_ref=stage.at[r, p, pl.ds(h * short, short)], dst_ref=final.at[way, tm, p],
            send_sem=tsend.at[r, p, h], recv_sem=frecv.at[way, tm, p],
            device_id=dev(r, h, blk), device_id_type=mesh_id)

    def send_block(r, way, has_before, p):
        nxt = z + 1 - 2 * way
        part[...] = corr(p)

        @pl.when(has_before)
        def _():
            pltpu.make_async_copy(transit.at[r, p], transit.at[r, p], trecv.at[r, p]).wait()
            part[...] += decode(transit.at[r, p], rows_run)

        @pl.when(r == nxt)
        def _():
            for h in range(2):
                encode(stage.at[r, p], h * short, part[h * rows:(h + 1) * rows, :])
                deliver(r, p, h).start()

        @pl.when(r != nxt)
        def _():
            encode(stage.at[r, p], 0, part[...])
            pass_on(r, p).start()

    def away(r, p):
        send_block(r, flip, zz > 0, p)

    def back(r, p):
        send_block(r, 1 - flip, zz < n_run - 1, p)

    n_wide = half // WIDE
    farthest = unflip(n_run - 1)
    late = (zz > 0).astype(jnp.int32)

    def pair(p, carry):
        @pl.when(p < n_wide)
        def _():
            lane0 = pl.multiple_of(p * WIDE, WIDE)
            lag = jnp.concatenate([lagscr[pl.ds(2 * p, 1), :], lagscr[pl.ds(2 * p + 1, 1), :]], axis=1)

            def store(r0, g, v):
                scores[r0:r0 + CHUNK, pl.ds(pl.multiple_of(lane0 + g * 128, 128), 128)] = v

            normalize(xfull, pl.ds(lane0, WIDE), lag, store)

        t = p - late

        @pl.when(t == 0)
        def _():
            prepare(farthest)

        @pl.when(jnp.logical_and(t >= 0, t < n_wide))
        def _():
            away(farthest, t)

        return carry

    lax.fori_loop(0, n_wide + 1, pair, 0)

    def all_wide(send, r):
        prepare(r)

        def wide(p, carry):
            send(r, p)
            return carry

        lax.fori_loop(0, n_wide, wide, 0)

    in_order(lambda r: all_wide(away, r), lambda r: all_wide(back, r), skip=True)

    prepare(z)
    for p in range(n_wide):
        own[:, p * WIDE:(p + 1) * WIDE] = corr(p)
    keep = pl.ds(pl.multiple_of(tm * rows, rows), rows)
    give = pl.ds(pl.multiple_of(other * rows, rows), rows)
    trade = pltpu.make_async_remote_copy(
        src_ref=own.at[give, :], dst_ref=ownrecv, send_sem=osem.at[0], recv_sem=osem.at[1],
        device_id=dev(z, other, blk), device_id_type=mesh_id)
    trade.start()
    out_ref[:, mine] = own[keep, :] / n_run
    trade.wait_recv()
    out_ref[:, theirs] = ownrecv[...] / n_run
    for way, present in ((0, z > 0), (1, z < n_run - 1)):

        @pl.when(present)
        def _():
            for p in range(n_wide):
                for c in range(2):
                    pltpu.make_async_copy(final.at[way, c, p], final.at[way, c, p], frecv.at[way, c, p]).wait()
                    cols = slice(c * half + p * WIDE, c * half + (p + 1) * WIDE)
                    out_ref[:, cols] += decode(final.at[way, c, p], rows) / n_run

    sswap.wait_send()
    swap.wait_send()
    trade.wait_send()

    def drain(r, carry):
        for d in range(1, n_blk):
            seed_copy(d, r).wait_send()

        next_door = jnp.logical_or(r == z - 1, r == z + 1)

        @pl.when(next_door)
        def _():
            for p in range(n_wide):
                for h in range(2):
                    deliver(r, p, h).wait_send()

        @pl.when(jnp.logical_and(r != z, jnp.logical_not(next_door)))
        def _():
            for p in range(n_wide):
                pass_on(r, p).wait_send()

        return carry

    lax.fori_loop(0, n_run, drain, 0)


def local(n_run, n_blk, series, weights, taps, lags):
    signal = series[0]
    frames, panel = signal.shape
    half = panel // 2
    fp = -(-2 * frames // 256) * 256
    n_filter = -(-(fp + LAGS) // OUT_BLK)
    rows_run = SEED_DEV // n_run * n_blk
    rows = rows_run // 2
    long, short = 2 * rows_run + 16, 2 * rows + 16
    n_wide = half // WIDE
    vmem = pl.BlockSpec(memory_space=pltpu.VMEM)
    dma = pltpu.SemaphoreType.DMA
    f32, b16 = jnp.float32, jnp.bfloat16
    flops = 2 * half * fp * (IN_BLK + n_blk * SEED_DEV)
    return pl.pallas_call(
        functools.partial(kernel, (n_run, n_blk, frames, panel, fp, n_filter)),
        out_shape=jax.ShapeDtypeStruct((rows, panel), f32),
        in_specs=[pl.BlockSpec(memory_space=pl.ANY), vmem, pl.BlockSpec(memory_space=pltpu.SMEM), vmem],
        out_specs=vmem,
        scratch_shapes=[
            pltpu.VMEM((frames, panel), b16),
            pltpu.VMEM((frames, SEED_DEV), b16),
            pltpu.VMEM((frames, SEED_DEV), b16),
            pltpu.VMEM((n_filter * OUT_BLK + IN_BLK - OUT_BLK, SEED_DEV), f32),
            pltpu.VMEM((fp, SEED_DEV), b16),
            pltpu.VMEM((frames, half), b16),
            pltpu.VMEM((n_filter * OUT_BLK + IN_BLK - OUT_BLK, half), f32),
            pltpu.VMEM((OUT_BLK, IN_BLK), b16),
            pltpu.VMEM((fp, 128), f32),
            pltpu.VMEM((fp, 128), f32),
            pltpu.VMEM((half // 128, 128), jnp.int32),
            pltpu.VMEM((n_filter * OUT_BLK, 256), f32),
            pltpu.VMEM((fp, 256), f32),
            pltpu.VMEM((fp, half), b16),
            pltpu.VMEM((n_blk, n_run, SEED_DEV // n_run, fp), b16),
            pltpu.VMEM((rows_run, fp), b16),
            pltpu.VMEM((n_run, n_wide, 2 * short, 128), jnp.int16),
            pltpu.VMEM((n_run, n_wide, long, 128), jnp.int16),
            pltpu.VMEM((2, 2, n_wide, short, 128), jnp.int16),
            pltpu.VMEM((rows_run, WIDE), f32),
            pltpu.VMEM((rows_run, half), f32),
            pltpu.VMEM((rows, half), f32),
            dma((5,)),
            dma((n_blk, n_run)),
            dma((n_blk, n_run)),
            dma((n_run, n_wide, 2)),
            dma((n_run, n_wide)),
            dma((2, 2, n_wide)),
            dma((2,)),
        ],
        compiler_params=pltpu.CompilerParams(
            collective_id=0, has_side_effects=True, vmem_limit_bytes=56 * 1024 * 1024),
        cost_estimate=pl.CostEstimate(flops=flops, bytes_accessed=2 * frames * panel, transcendentals=0),
    )(signal, weights, taps, lags.reshape(panel // 128, 128))


def solution(mesh):
    placed = (P("run", "tm", "blk"), P("run", None), P(), P("blk"))
    body = functools.partial(local, mesh.shape["run"], mesh.shape["blk"])
    return jax.shard_map(
        body, mesh=mesh, in_specs=placed, out_specs=P(("run", "tm"), "blk"), check_vma=False
    )
```

time: 33.8 us -> 33.4 us (0.988)
  other arithmetic: 1.17 us -> 0 us
  Pallas kernels: 30.6 us -> 31.4 us
    convert_element_type x1 -> x0, other arithmetic: 1.17 us -> none  [local(): taps.astype(f32)]
    pallas_call x1, Pallas kernels: 30.6 us -> 31.4 us  [local(): pl.pallas_call(functools.partial(kernel, (n_run, n_blk, frames, panel, fp...]
where the time goes in v3:
time: 33.4 us; the launch traced here: 33.2 us
  Pallas kernels  31.4 us (94%)
  local copies, waits for them, and re-layouts  1.77 us (5%)
    pallas_call x1, Pallas kernels, local(): pl.pallas_call(functools.partial(kernel, (n_run, n_blk, frames, panel, fp...  31.4 us
    unnamed x1, local copies, waits for them, and re-layouts  1.77 us

profile of v3, /device:TPU:19, one launch (start us, length us, event | category | flops | bytes accessed | tf_op | source)
XLA Modules:
  0.0 33.2 jit_solution(16180800081818896752)
XLA Ops:
  0.0 31.4 %shard_map.46 = f32[64,1536]{1,0:T(8,128)} custom-call(bf16[600,1536]{1,0:T(8,128)(2,1)} %bitcast.2, s32[1,1200]{1,0:T(1,128)} %w_ref.1, bf16[33]{0:T(256)(128)(2,1)} %taps_ref.1, s32[12,128]{1,0:T(8,128)} %bitcast.3), custom_call_target="tpu_custom_call" | custom-call | flops 1509949440 | bytes 1843200 | tf_op jit(solution)/shard_map/pallas_call | solution.py:376
  31.4 1.8 %copy.6 = f32[64,1536]{1,0:T(8,128)} copy(f32[64,1536]{1,0:T(8,128)} %shard_map.46) | data formatting | bytes 786432

commit v4 on v3

--- a/solution.py
+++ b/solution.py
@@ -21,7 +21,7 @@
 
 
 def kernel(dims, x_hbm, w_ref, taps_ref, lags_ref, out_ref, x_ref, sown, sother, sfull, sscore, xrecv, xfull, toep, wcol,
-           rcol, lagscr, banded, filt, scores, seeds, left, stage, transit, final, part, own, ownrecv, xsem, dsend, srecv, tsend,
+           rcol, lagscr, banded, filt, scores, seeds, left, stage, transit, final, part, own, ownrecv, xsem, dsend, fsend, srecv, tsend,
            trecv, frecv, osem):
     n_run, n_blk, frames, panel, fp, n_filter = dims
     half = panel // 2
@@ -160,33 +160,39 @@
     def unflip(rr):
         return rr + flip * (n_run - 1 - 2 * rr)
 
-    def in_order(out, home, skip=False):
-        def step(k, carry):
-            far = n_run - 1 - k
-
-            @pl.when(jnp.logical_and(far > zz, k > 0) if skip else far > zz)
-            def _():
-                out(unflip(far))
-
-            @pl.when(k < zz)
-            def _():
-                home(unflip(k))
-
-            return carry
-
-        lax.fori_loop(0, n_run, step, 0)
+    def turn(j):
+        pairs = jnp.where(lax.rem(j, 2) == 0, n_run - 1 - lax.div(j, 2), lax.div(j, 2))
+        return unflip(jnp.where(j < 2 * zz, pairs, n_run - 1 - j + zz))
+
+    farthest = unflip(n_run - 1)
 
     def seed_copy(d, r):
         return pltpu.make_async_remote_copy(
             src_ref=seeds.at[blk, r], dst_ref=seeds.at[blk, r], send_sem=dsend.at[d, r],
             recv_sem=srecv.at[blk, r], device_id=dev(z, tm, lax.rem(blk + d, n_blk)), device_id_type=mesh_id)
 
-    def send_seeds(r):
-        for d in range(1, n_blk):
-            seed_copy(d, r).start()
-
-    in_order(send_seeds, send_seeds)
-    send_seeds(z)
+    def relay_copy(d, r):
+        peer = lax.rem(blk + n_blk - d, n_blk)
+        return pltpu.make_async_remote_copy(
+            src_ref=seeds.at[peer, r], dst_ref=seeds.at[peer, r], send_sem=fsend.at[d, r],
+            recv_sem=srecv.at[peer, r], device_id=dev(z, other, blk), device_id_type=mesh_id)
+
+    def arrived(d, r):
+        peer = lax.rem(blk + n_blk - d, n_blk)
+        pltpu.make_async_copy(seeds.at[peer, r], seeds.at[peer, r], srecv.at[peer, r]).wait()
+
+    def carried(r):
+        return jnp.logical_and(r != farthest, lax.rem(r, 2) == tm)
+
+    def relay(r):
+        @pl.when(carried(r))
+        def _():
+            for d in range(1, n_blk):
+                arrived(d, r)
+                relay_copy(d, r).start()
+
+    for d in range(1, n_blk):
+        seed_copy(d, farthest).start()
 
     swap.wait_recv()
     xfull[far_rows, :] = xrecv[...].astype(jnp.float32)
@@ -201,9 +207,11 @@
     order = one_hot(j == lax.rem(i, n_vec) * q_run + lax.div(i, n_vec))
 
     def prepare(r):
-        for d in range(1, n_blk):
-            peer = lax.rem(blk + d, n_blk)
-            pltpu.make_async_copy(seeds.at[peer, r], seeds.at[peer, r], srecv.at[peer, r]).wait()
+        @pl.when(jnp.logical_not(carried(r)))
+        def _():
+            for d in range(1, n_blk):
+                arrived(d, r)
+
         rows_left = jnp.concatenate([seeds[b, r] for b in range(n_blk)], axis=0)
         left[...] = jnp.dot(order, rows_left, preferred_element_type=jnp.float32).astype(jnp.bfloat16)
 
@@ -245,34 +253,36 @@
             send_sem=tsend.at[r, p, h], recv_sem=frecv.at[way, tm, p],
             device_id=dev(r, h, blk), device_id_type=mesh_id)
 
-    def send_block(r, way, has_before, p):
-        nxt = z + 1 - 2 * way
+    def send_block(r, p):
+        up = r > z
+        nxt = jnp.where(up, z + 1, z - 1)
         part[...] = corr(p)
 
-        @pl.when(has_before)
+        @pl.when(jnp.logical_or(jnp.logical_and(up, z > 0), jnp.logical_and(r < z, z < n_run - 1)))
         def _():
             pltpu.make_async_copy(transit.at[r, p], transit.at[r, p], trecv.at[r, p]).wait()
             part[...] += decode(transit.at[r, p], rows_run)
 
+        def after():
+            @pl.when(jnp.logical_and(r != 0, r != n_run - 1))
+            def _():
+                pass_on(jnp.where(up, r + 1, r - 1), p).wait_send()
+
         @pl.when(r == nxt)
         def _():
             for h in range(2):
                 encode(stage.at[r, p], h * short, part[h * rows:(h + 1) * rows, :])
+            after()
+            for h in range(2):
                 deliver(r, p, h).start()
 
         @pl.when(r != nxt)
         def _():
             encode(stage.at[r, p], 0, part[...])
+            after()
             pass_on(r, p).start()
 
-    def away(r, p):
-        send_block(r, flip, zz > 0, p)
-
-    def back(r, p):
-        send_block(r, 1 - flip, zz < n_run - 1, p)
-
     n_wide = half // WIDE
-    farthest = unflip(n_run - 1)
     late = (zz > 0).astype(jnp.int32)
 
     def pair(p, carry):
@@ -286,6 +296,20 @@
 
             normalize(xfull, pl.ds(lane0, WIDE), lag, store)
 
+        @pl.when(p == 0)
+        def _():
+            def send_rest(j, carry):
+                r = turn(j)
+
+                @pl.when(carried(r))
+                def _():
+                    for d in range(1, n_blk):
+                        seed_copy(d, r).start()
+
+                return carry
+
+            lax.fori_loop(1, n_run, send_rest, 0)
+
         t = p - late
 
         @pl.when(t == 0)
@@ -294,22 +318,30 @@
 
         @pl.when(jnp.logical_and(t >= 0, t < n_wide))
         def _():
-            away(farthest, t)
+            send_block(farthest, t)
 
         return carry
 
     lax.fori_loop(0, n_wide + 1, pair, 0)
 
-    def all_wide(send, r):
+    relay(turn(1))
+
+    def send_run(j, carry):
+        r = turn(j)
         prepare(r)
 
         def wide(p, carry):
-            send(r, p)
+            @pl.when(p == n_wide - 1)
+            def _():
+                relay(turn(j + 1))
+
+            send_block(r, p)
             return carry
 
         lax.fori_loop(0, n_wide, wide, 0)
-
-    in_order(lambda r: all_wide(away, r), lambda r: all_wide(back, r), skip=True)
+        return carry
+
+    lax.fori_loop(1, n_run - 1, send_run, 0)
 
     prepare(z)
     for p in range(n_wide):
@@ -338,21 +370,21 @@
     trade.wait_send()
 
     def drain(r, carry):
-        for d in range(1, n_blk):
-            seed_copy(d, r).wait_send()
-
-        next_door = jnp.logical_or(r == z - 1, r == z + 1)
-
-        @pl.when(next_door)
+        @pl.when(jnp.logical_or(carried(r), r == farthest))
+        def _():
+            for d in range(1, n_blk):
+                seed_copy(d, r).wait_send()
+
+        @pl.when(carried(r))
+        def _():
+            for d in range(1, n_blk):
+                relay_copy(d, r).wait_send()
+
+        @pl.when(jnp.logical_or(r == z - 1, r == z + 1))
         def _():
             for p in range(n_wide):
                 for h in range(2):
                     deliver(r, p, h).wait_send()
-
-        @pl.when(jnp.logical_and(r != z, jnp.logical_not(next_door)))
-        def _():
-            for p in range(n_wide):
-                pass_on(r, p).wait_send()
 
         return carry
 
@@ -404,6 +436,7 @@
             dma((5,)),
             dma((n_blk, n_run)),
             dma((n_blk, n_run)),
+            dma((n_blk, n_run)),
             dma((n_run, n_wide, 2)),
             dma((n_run, n_wide)),
             dma((2, 2, n_wide)),

time: 33.4 us -> 34.7 us (1.039)
  Pallas kernels: 31.4 us -> 32.7 us
    pallas_call x1, Pallas kernels: 31.4 us -> 32.7 us  [local(): pl.pallas_call(functools.partial(kernel, (n_run, n_blk, frames, panel, fp...]
where the time goes in v4:
time: 34.7 us; the launch traced here: 34.5 us
  Pallas kernels  32.7 us (94%)
  local copies, waits for them, and re-layouts  1.77 us (5%)
    pallas_call x1, Pallas kernels, local(): pl.pallas_call(functools.partial(kernel, (n_run, n_blk, frames, panel, fp...  32.7 us
    unnamed x1, local copies, waits for them, and re-layouts  1.77 us

profile of v4, /device:TPU:19, one launch (start us, length us, event | category | flops | bytes accessed | tf_op | source)
XLA Modules:
  0.0 34.5 jit_solution(9851768488879957038)
XLA Ops:
  0.0 32.7 %shard_map.46 = f32[64,1536]{1,0:T(8,128)} custom-call(bf16[600,1536]{1,0:T(8,128)(2,1)} %bitcast.2, s32[1,1200]{1,0:T(1,128)} %w_ref.1, bf16[33]{0:T(256)(128)(2,1)} %taps_ref.1, s32[12,128]{1,0:T(8,128)} %bitcast.3), custom_call_target="tpu_custom_call" | custom-call | flops 1509949440 | bytes 1843200 | tf_op jit(solution)/shard_map/pallas_call | solution.py:408
  32.7 1.8 %copy.6 = f32[64,1536]{1,0:T(8,128)} copy(f32[64,1536]{1,0:T(8,128)} %shard_map.46) | data formatting | bytes 786432

commit v5 on v4

--- a/solution.py
+++ b/solution.py
@@ -21,7 +21,7 @@
 
 
 def kernel(dims, x_hbm, w_ref, taps_ref, lags_ref, out_ref, x_ref, sown, sother, sfull, sscore, xrecv, xfull, toep, wcol,
-           rcol, lagscr, banded, filt, scores, seeds, left, stage, transit, final, part, own, ownrecv, xsem, dsend, fsend, srecv, tsend,
+           rcol, lagscr, banded, filt, scores, seeds, left, stage, transit, final, part, own, ownrecv, xsem, dsend, srecv, tsend,
            trecv, frecv, osem):
     n_run, n_blk, frames, panel, fp, n_filter = dims
     half = panel // 2
@@ -62,21 +62,6 @@
     load = pltpu.make_async_copy(x_hbm, x_ref, xsem.at[4])
     load.start()
 
-    diff = (lax.broadcasted_iota(jnp.int32, (OUT_BLK, IN_BLK), 1)
-            - lax.broadcasted_iota(jnp.int32, (OUT_BLK, IN_BLK), 0))
-    band = jnp.zeros((OUT_BLK, IN_BLK), jnp.float32)
-    for k in range(TAPS):
-        band = jnp.where(diff == k, taps_ref[k].astype(jnp.float32), band)
-    toep[...] = band.astype(jnp.bfloat16)
-
-    wrow = w_ref[...].astype(jnp.float32)
-    total = jnp.sum(wrow)
-    wrow = jnp.concatenate([wrow, jnp.zeros((1, fp - total_frames), jnp.float32)], axis=1)
-    for j in range(fp // 128):
-        square = jnp.broadcast_to(wrow[:, j * 128:(j + 1) * 128], (128, 128)).T
-        wcol[j * 128:(j + 1) * 128, :] = square
-        rcol[j * 128:(j + 1) * 128, :] = jnp.sqrt(square)
-
     def one_hot(mask):
         return mask.astype(jnp.float32).astype(jnp.bfloat16)
 
@@ -96,6 +81,21 @@
         src_ref=x_ref.at[:, theirs], dst_ref=xrecv, send_sem=xsem.at[0], recv_sem=xsem.at[1],
         device_id=dev(z, other, blk), device_id_type=mesh_id)
     swap.start()
+
+    lane = lax.broadcasted_iota(jnp.int32, (8, IN_BLK), 1)
+    row = jnp.zeros((8, IN_BLK), jnp.float32)
+    for k in range(TAPS):
+        row = jnp.where(lane == k, taps_ref[k].astype(jnp.float32), row)
+    band = jnp.broadcast_to(row[0:1, :], (OUT_BLK, IN_BLK))
+    toep[...] = pltpu.roll(band, 0, 1, stride=1, stride_axis=0).astype(jnp.bfloat16)
+
+    wrow = w_ref[...].astype(jnp.float32)
+    total = jnp.sum(wrow)
+    wrow = jnp.concatenate([wrow, jnp.zeros((1, fp - total_frames), jnp.float32)], axis=1)
+    for j in range(fp // 128):
+        square = jnp.broadcast_to(wrow[:, j * 128:(j + 1) * 128], (128, 128)).T
+        wcol[j * 128:(j + 1) * 128, :] = square
+        rcol[j * 128:(j + 1) * 128, :] = jnp.sqrt(square)
 
     tail = HALF + total_frames
     near = pl.ds(pl.multiple_of(HALF + tm * frames, 8), frames)
@@ -171,28 +171,15 @@
             src_ref=seeds.at[blk, r], dst_ref=seeds.at[blk, r], send_sem=dsend.at[d, r],
             recv_sem=srecv.at[blk, r], device_id=dev(z, tm, lax.rem(blk + d, n_blk)), device_id_type=mesh_id)
 
-    def relay_copy(d, r):
-        peer = lax.rem(blk + n_blk - d, n_blk)
-        return pltpu.make_async_remote_copy(
-            src_ref=seeds.at[peer, r], dst_ref=seeds.at[peer, r], send_sem=fsend.at[d, r],
-            recv_sem=srecv.at[peer, r], device_id=dev(z, other, blk), device_id_type=mesh_id)
-
     def arrived(d, r):
         peer = lax.rem(blk + n_blk - d, n_blk)
         pltpu.make_async_copy(seeds.at[peer, r], seeds.at[peer, r], srecv.at[peer, r]).wait()
 
-    def carried(r):
-        return jnp.logical_and(r != farthest, lax.rem(r, 2) == tm)
-
-    def relay(r):
-        @pl.when(carried(r))
-        def _():
-            for d in range(1, n_blk):
-                arrived(d, r)
-                relay_copy(d, r).start()
-
-    for d in range(1, n_blk):
-        seed_copy(d, farthest).start()
+    def send_seeds(r):
+        for d in range(1, n_blk):
+            seed_copy(d, r).start()
+
+    send_seeds(farthest)
 
     swap.wait_recv()
     xfull[far_rows, :] = xrecv[...].astype(jnp.float32)
@@ -207,11 +194,8 @@
     order = one_hot(j == lax.rem(i, n_vec) * q_run + lax.div(i, n_vec))
 
     def prepare(r):
-        @pl.when(jnp.logical_not(carried(r)))
-        def _():
-            for d in range(1, n_blk):
-                arrived(d, r)
-
+        for d in range(1, n_blk):
+            arrived(d, r)
         rows_left = jnp.concatenate([seeds[b, r] for b in range(n_blk)], axis=0)
         left[...] = jnp.dot(order, rows_left, preferred_element_type=jnp.float32).astype(jnp.bfloat16)
 
@@ -298,17 +282,7 @@
 
         @pl.when(p == 0)
         def _():
-            def send_rest(j, carry):
-                r = turn(j)
-
-                @pl.when(carried(r))
-                def _():
-                    for d in range(1, n_blk):
-                        seed_copy(d, r).start()
-
-                return carry
-
-            lax.fori_loop(1, n_run, send_rest, 0)
+            send_seeds(turn(1))
 
         t = p - late
 
@@ -324,17 +298,18 @@
 
     lax.fori_loop(0, n_wide + 1, pair, 0)
 
-    relay(turn(1))
+    send_seeds(turn(2))
 
     def send_run(j, carry):
         r = turn(j)
+
+        @pl.when(j + 2 < n_run)
+        def _():
+            send_seeds(turn(j + 2))
+
         prepare(r)
 
         def wide(p, carry):
-            @pl.when(p == n_wide - 1)
-            def _():
-                relay(turn(j + 1))
-
             send_block(r, p)
             return carry
 
@@ -370,15 +345,8 @@
     trade.wait_send()
 
     def drain(r, carry):
-        @pl.when(jnp.logical_or(carried(r), r == farthest))
-        def _():
-            for d in range(1, n_blk):
-                seed_copy(d, r).wait_send()
-
-        @pl.when(carried(r))
-        def _():
-            for d in range(1, n_blk):
-                relay_copy(d, r).wait_send()
+        for d in range(1, n_blk):
+            seed_copy(d, r).wait_send()
 
         @pl.when(jnp.logical_or(r == z - 1, r == z + 1))
         def _():
@@ -407,7 +375,7 @@
     flops = 2 * half * fp * (IN_BLK + n_blk * SEED_DEV)
     return pl.pallas_call(
         functools.partial(kernel, (n_run, n_blk, frames, panel, fp, n_filter)),
-        out_shape=jax.ShapeDtypeStruct((rows, panel), f32),
+        out_shape=pltpu.VMEM((rows, panel), f32),
         in_specs=[pl.BlockSpec(memory_space=pl.ANY), vmem, pl.BlockSpec(memory_space=pltpu.SMEM), vmem],
         out_specs=vmem,
         scratch_shapes=[
@@ -436,7 +404,6 @@
             dma((5,)),
             dma((n_blk, n_run)),
             dma((n_blk, n_run)),
-            dma((n_blk, n_run)),
             dma((n_run, n_wide, 2)),
             dma((n_run, n_wide)),
             dma((2, 2, n_wide)),

time: 34.7 us -> 34.7 us (level)
  the two profiles are of different devices: /device:TPU:19 before, /device:TPU:9 now
where the time goes in v5:
time: 34.7 us; the launch traced here: 34.5 us
  Pallas kernels  33.7 us (97%)
  local copies, waits for them, and re-layouts  0.75 us (2%)
    pallas_call x1, Pallas kernels, local(): pl.pallas_call(functools.partial(kernel, (n_run, n_blk, frames, panel, fp...  33.7 us
    unnamed x1, local copies, waits for them, and re-layouts  0.75 us

profile of v5, /device:TPU:9, one launch (start us, length us, event | category | flops | bytes accessed | tf_op | source)
XLA Modules:
  0.0 34.5 jit_solution(14206840501282723216)
XLA Ops:
  0.0 33.7 %shard_map.46 = f32[64,1536]{1,0:T(8,128)S(1)} custom-call(bf16[600,1536]{1,0:T(8,128)(2,1)} %bitcast.2, s32[1,1200]{1,0:T(1,128)} %w_ref.1, bf16[33]{0:T(256)(128)(2,1)} %taps_ref.1, s32[12,128]{1,0:T(8,128)} %bitcast.3), custom_call_target="tpu_custom_call" | custom-call | flops 1509949440 | bytes 1843200 | tf_op jit(solution)/shard_map/pallas_call | solution.py:376
  33.7 0.7 %copy.6 = f32[64,1536]{1,0:T(8,128)} copy(f32[64,1536]{1,0:T(8,128)S(1)} %shard_map.46) | data formatting | bytes 786432

commit v6 on v5

--- a/solution.py
+++ b/solution.py
@@ -62,6 +62,14 @@
     load = pltpu.make_async_copy(x_hbm, x_ref, xsem.at[4])
     load.start()
 
+    wrow = w_ref[...].astype(jnp.float32)
+    total = jnp.sum(wrow)
+    wrow = jnp.concatenate([wrow, jnp.zeros((1, fp - total_frames), jnp.float32)], axis=1)
+    for j in range(fp // 128):
+        square = jnp.broadcast_to(wrow[:, j * 128:(j + 1) * 128], (128, 128)).T
+        wcol[j * 128:(j + 1) * 128, :] = square
+        rcol[j * 128:(j + 1) * 128, :] = jnp.sqrt(square)
+
     def one_hot(mask):
         return mask.astype(jnp.float32).astype(jnp.bfloat16)
 
@@ -88,14 +96,6 @@
         row = jnp.where(lane == k, taps_ref[k].astype(jnp.float32), row)
     band = jnp.broadcast_to(row[0:1, :], (OUT_BLK, IN_BLK))
     toep[...] = pltpu.roll(band, 0, 1, stride=1, stride_axis=0).astype(jnp.bfloat16)
-
-    wrow = w_ref[...].astype(jnp.float32)
-    total = jnp.sum(wrow)
-    wrow = jnp.concatenate([wrow, jnp.zeros((1, fp - total_frames), jnp.float32)], axis=1)
-    for j in range(fp // 128):
-        square = jnp.broadcast_to(wrow[:, j * 128:(j + 1) * 128], (128, 128)).T
-        wcol[j * 128:(j + 1) * 128, :] = square
-        rcol[j * 128:(j + 1) * 128, :] = jnp.sqrt(square)
 
     tail = HALF + total_frames
     near = pl.ds(pl.multiple_of(HALF + tm * frames, 8), frames)
@@ -138,8 +138,6 @@
     lag_all = jnp.broadcast_to(jnp.concatenate(lag_rows, axis=1), (8, panel)).astype(jnp.float32)
     seed_lag = jnp.dot(lag_all.astype(jnp.bfloat16), pick, preferred_element_type=jnp.float32)
     seed_lag = seed_lag.astype(jnp.int32)[0:1, :]
-    edges(xfull, half)
-    xfull[near, :] = x_ref[:, mine].astype(jnp.float32)
     sswap.wait_recv()
     sfull[far_rows, :] = sother[...].astype(jnp.float32)
 
@@ -181,6 +179,8 @@
 
     send_seeds(farthest)
 
+    edges(xfull, half)
+    xfull[near, :] = x_ref[:, mine].astype(jnp.float32)
     swap.wait_recv()
     xfull[far_rows, :] = xrecv[...].astype(jnp.float32)
     lag_own = jnp.where(tm == 0, jnp.concatenate(lag_rows[:groups], axis=1),
@@ -284,6 +284,14 @@
         def _():
             send_seeds(turn(1))
 
+        @pl.when(p == 1)
+        def _():
+            def send_rest(j, carry):
+                send_seeds(turn(j))
+                return carry
+
+            lax.fori_loop(2, n_run, send_rest, 0)
+
         t = p - late
 
         @pl.when(t == 0)
@@ -297,15 +305,9 @@
         return carry
 
     lax.fori_loop(0, n_wide + 1, pair, 0)
-
-    send_seeds(turn(2))
 
     def send_run(j, carry):
         r = turn(j)
-
-        @pl.when(j + 2 < n_run)
-        def _():
-            send_seeds(turn(j + 2))
 
         prepare(r)
 

time: 34.7 us -> 31.2 us (0.90)
  the two profiles are of different devices: /device:TPU:9 before, /device:TPU:19 now
where the time goes in v6:
time: 31.2 us; the launch traced here: 31 us
  Pallas kernels  30.3 us (97%)
  local copies, waits for them, and re-layouts  0.75 us (2%)
    pallas_call x1, Pallas kernels, local(): pl.pallas_call(functools.partial(kernel, (n_run, n_blk, frames, panel, fp...  30.3 us
    unnamed x1, local copies, waits for them, and re-layouts  0.75 us

profile of v6, /device:TPU:19, one launch (start us, length us, event | category | flops | bytes accessed | tf_op | source)
XLA Modules:
  0.0 31.0 jit_solution(15015955797665350089)
XLA Ops:
  0.0 30.3 %shard_map.46 = f32[64,1536]{1,0:T(8,128)S(1)} custom-call(bf16[600,1536]{1,0:T(8,128)(2,1)} %bitcast.2, s32[1,1200]{1,0:T(1,128)} %w_ref.1, bf16[33]{0:T(256)(128)(2,1)} %taps_ref.1, s32[12,128]{1,0:T(8,128)} %bitcast.3), custom_call_target="tpu_custom_call" | custom-call | flops 1509949440 | bytes 1843200 | tf_op jit(solution)/shard_map/pallas_call | solution.py:378
  30.3 0.7 %copy.6 = f32[64,1536]{1,0:T(8,128)} copy(f32[64,1536]{1,0:T(8,128)S(1)} %shard_map.46) | data formatting | bytes 786432

commit v7 on v6

--- a/solution.py
+++ b/solution.py
@@ -20,7 +20,7 @@
 epsilon = 1e-05
 
 
-def kernel(dims, x_hbm, w_ref, taps_ref, lags_ref, out_ref, x_ref, sown, sother, sfull, sscore, xrecv, xfull, toep, wcol,
+def kernel(dims, x_hbm, w_hbm, taps_hbm, lags_hbm, out_ref, w_ref, taps_ref, lags_ref, x_ref, sown, sother, sfull, sscore, xrecv, xfull, toep, wcol,
            rcol, lagscr, banded, filt, scores, seeds, left, stage, transit, final, part, own, ownrecv, xsem, dsend, srecv, tsend,
            trecv, frecv, osem):
     n_run, n_blk, frames, panel, fp, n_filter = dims
@@ -59,8 +59,15 @@
 
     mine = pl.ds(pl.multiple_of(tm * half, 128), half)
     theirs = pl.ds(pl.multiple_of(other * half, 128), half)
-    load = pltpu.make_async_copy(x_hbm, x_ref, xsem.at[4])
-    load.start()
+    loads = [pltpu.make_async_copy(w_hbm, w_ref, xsem.at[4])]
+    for c in range(2):
+        cols = slice(c * half, (c + 1) * half)
+        loads.append(pltpu.make_async_copy(x_hbm.at[:, cols], x_ref.at[:, cols], xsem.at[5 + c]))
+    loads.append(pltpu.make_async_copy(taps_hbm, taps_ref, xsem.at[7]))
+    loads.append(pltpu.make_async_copy(lags_hbm, lags_ref, xsem.at[8]))
+    for load in loads:
+        load.start()
+    loads[0].wait()
 
     wrow = w_ref[...].astype(jnp.float32)
     total = jnp.sum(wrow)
@@ -75,8 +82,12 @@
 
     pick = one_hot(lax.broadcasted_iota(jnp.int32, (panel, SEED_DEV), 0)
                    == (panel // SEED_DEV) * lax.broadcasted_iota(jnp.int32, (panel, SEED_DEV), 1))
-    load.wait()
-    sown[...] = jnp.dot(x_ref[...], pick, preferred_element_type=jnp.float32).astype(jnp.bfloat16)
+    picked = jnp.zeros((frames, SEED_DEV), jnp.float32)
+    for c in range(2):
+        loads[1 + c].wait()
+        cols = slice(c * half, (c + 1) * half)
+        picked = picked + jnp.dot(x_ref[:, cols], pick[cols], preferred_element_type=jnp.float32)
+    sown[...] = picked.astype(jnp.bfloat16)
 
     inner = jnp.logical_and(z > 0, z < n_run - 1)
     pl.semaphore_wait(barrier, jnp.where(inner, n_blk + 4, n_blk + 2))
@@ -90,6 +101,8 @@
         device_id=dev(z, other, blk), device_id_type=mesh_id)
     swap.start()
 
+    loads[3].wait()
+    loads[4].wait()
     lane = lax.broadcasted_iota(jnp.int32, (8, IN_BLK), 1)
     row = jnp.zeros((8, IN_BLK), jnp.float32)
     for k in range(TAPS):
@@ -267,24 +280,26 @@
             pass_on(r, p).start()
 
     n_wide = half // WIDE
-    late = (zz > 0).astype(jnp.int32)
+    begin = jnp.where(zz > 0, n_wide - 1, min(1, n_wide - 1))
+
+    def send_farthest(t, carry):
+        send_block(farthest, t)
+        return carry
 
     def pair(p, carry):
-        @pl.when(p < n_wide)
-        def _():
-            lane0 = pl.multiple_of(p * WIDE, WIDE)
-            lag = jnp.concatenate([lagscr[pl.ds(2 * p, 1), :], lagscr[pl.ds(2 * p + 1, 1), :]], axis=1)
-
-            def store(r0, g, v):
-                scores[r0:r0 + CHUNK, pl.ds(pl.multiple_of(lane0 + g * 128, 128), 128)] = v
-
-            normalize(xfull, pl.ds(lane0, WIDE), lag, store)
+        lane0 = pl.multiple_of(p * WIDE, WIDE)
+        lag = jnp.concatenate([lagscr[pl.ds(2 * p, 1), :], lagscr[pl.ds(2 * p + 1, 1), :]], axis=1)
+
+        def store(r0, g, v):
+            scores[r0:r0 + CHUNK, pl.ds(pl.multiple_of(lane0 + g * 128, 128), 128)] = v
+
+        normalize(xfull, pl.ds(lane0, WIDE), lag, store)
 
         @pl.when(p == 0)
         def _():
             send_seeds(turn(1))
 
-        @pl.when(p == 1)
+        @pl.when(p == min(1, n_wide - 1))
         def _():
             def send_rest(j, carry):
                 send_seeds(turn(j))
@@ -292,19 +307,17 @@
 
             lax.fori_loop(2, n_run, send_rest, 0)
 
-        t = p - late
-
-        @pl.when(t == 0)
+        @pl.when(p == begin)
         def _():
             prepare(farthest)
 
-        @pl.when(jnp.logical_and(t >= 0, t < n_wide))
-        def _():
-            send_block(farthest, t)
+        @pl.when(p >= begin)
+        def _():
+            lax.fori_loop(jnp.where(p == begin, 0, p), p + 1, send_farthest, 0)
 
         return carry
 
-    lax.fori_loop(0, n_wide + 1, pair, 0)
+    lax.fori_loop(0, n_wide, pair, 0)
 
     def send_run(j, carry):
         r = turn(j)
@@ -378,9 +391,12 @@
     return pl.pallas_call(
         functools.partial(kernel, (n_run, n_blk, frames, panel, fp, n_filter)),
         out_shape=pltpu.VMEM((rows, panel), f32),
-        in_specs=[pl.BlockSpec(memory_space=pl.ANY), vmem, pl.BlockSpec(memory_space=pltpu.SMEM), vmem],
+        in_specs=[pl.BlockSpec(memory_space=pl.ANY)] * 4,
         out_specs=vmem,
         scratch_shapes=[
+            pltpu.VMEM(weights.shape, jnp.int32),
+            pltpu.SMEM(taps.shape, b16),
+            pltpu.VMEM((panel // 128, 128), jnp.int32),
             pltpu.VMEM((frames, panel), b16),
             pltpu.VMEM((frames, SEED_DEV), b16),
             pltpu.VMEM((frames, SEED_DEV), b16),
@@ -403,7 +419,7 @@
             pltpu.VMEM((rows_run, WIDE), f32),
             pltpu.VMEM((rows_run, half), f32),
             pltpu.VMEM((rows, half), f32),
-            dma((5,)),
+            dma((9,)),
             dma((n_blk, n_run)),
             dma((n_blk, n_run)),
             dma((n_run, n_wide, 2)),

time: 31.2 us -> 30.3 us (0.971)
  Pallas kernels: 30.3 us -> 29.2 us
    pallas_call x1, Pallas kernels: 30.3 us -> 29.2 us  [local(): pl.pallas_call(functools.partial(kernel, (n_run, n_blk, frames, panel, fp...]
where the time goes in v7:
time: 30.3 us; the launch traced here: 30 us
  Pallas kernels  29.2 us (96%)
  local copies, waits for them, and re-layouts  0.75 us (2%)
    pallas_call x1, Pallas kernels, local(): pl.pallas_call(functools.partial(kernel, (n_run, n_blk, frames, panel, fp...  29.2 us
    unnamed x1, local copies, waits for them, and re-layouts  0.75 us

profile of v7, /device:TPU:19, one launch (start us, length us, event | category | flops | bytes accessed | tf_op | source)
XLA Modules:
  0.0 30.0 jit_solution(6507566518743053994)
XLA Ops:
  0.0 29.2 %shard_map.46 = f32[64,1536]{1,0:T(8,128)S(1)} custom-call(bf16[600,1536]{1,0:T(8,128)(2,1)} %bitcast.2, s32[1,1200]{1,0:T(1,128)} %w_hbm.1, bf16[33]{0:T(256)(128)(2,1)} %taps_hbm.1, s32[12,128]{1,0:T(8,128)} %bitcast.3), custom_call_target="tpu_custom_call" | custom-call | flops 1509949440 | bytes 1843200 | tf_op jit(solution)/shard_map/pallas_call | solution.py:391
  29.2 0.7 %copy.6 = f32[64,1536]{1,0:T(8,128)} copy(f32[64,1536]{1,0:T(8,128)S(1)} %shard_map.46) | data formatting | bytes 786432
